TPU v7x, 32 devices: a whole 2x2x4 slice. The times are simulated.
32 devices in a mesh: heads: 2 (over x), team: 2 (over core), blk: 8 (over z, y).
Axes of the slice: x: 2, y: 2, z: 4, core: 2. Of those that a mesh axis runs over, the one named last changes fastest.
Arguments:
- queries: bfloat16 [2, 512, 32, 128], P('heads', ('team', 'blk')), may hold values from -26 to 26
- keys: bfloat16 [2, 512, 8, 128], P('heads', ('team', 'blk')), may hold values from -26 to 26
- values: bfloat16 [2, 512, 8, 128], P('heads', ('team', 'blk')), may hold values from -6 to 6
- run_index: int32 [16], replicated, may hold values from 0 to 15, each once
Outputs:
- attended: bfloat16 [1024, 32, 128], P(('team', 'blk'), 'heads')
All inputs are finite; a program needn't handle non-finite values.
Results may differ from a plain program's by a relative error of at most 0.012.
The roundings to bfloat16 on the way count: a program that leaves them out, or rounds other values in their place, can miss the bound.
Values may be sent and summed in bfloat16 or wider, within the bound.
A program may use at most 64 MiB of HBM per device.

v0:
```python
import math

import jax
import jax.numpy as jnp
from jax import lax
from jax.sharding import PartitionSpec as P

mask_floor = -1e30
rope_theta = 500000.0
rope_factor = 8.0
low_factor = 1.0
high_factor = 4.0
initial_context = 8192.0


def inverse_freqs(head_width):
    half_width = head_width // 2
    counter = jnp.arange(half_width, dtype=jnp.float32)
    base_freq = 1.0 / rope_theta ** (2.0 * counter / head_width)
    wavelength = 2.0 * jnp.pi / base_freq
    smooth = (initial_context / wavelength - low_factor) / (high_factor - low_factor)
    blended = (1.0 - smooth) * base_freq / rope_factor + smooth * base_freq
    middle = jnp.where(wavelength > initial_context / low_factor, base_freq / rope_factor, blended)
    return jnp.where(wavelength < initial_context / high_factor, base_freq, middle)


def rotate_heads(values_in, positions, inverse):
    half_width = values_in.shape[-1] // 2
    angles = positions.astype(jnp.float32)[:, None] * inverse[None, :]
    cosine = jnp.cos(angles)[:, None, :]
    sine_part = jnp.sin(angles)[:, None, :]
    first_half = values_in[..., :half_width]
    second = values_in[..., half_width:]
    return jnp.concatenate(
        [first_half * cosine - second * sine_part, second * cosine + first_half * sine_part],
        axis=-1,
    )


def slot_positions(run_index, slot_ids, local_rows, half_rows):
    slot_count = run_index.shape[0]
    matches = slot_ids[:, None] == jnp.arange(slot_count, dtype=jnp.int32)[None, :]
    run_ids = jnp.sum(jnp.where(matches, run_index[None, :], 0), axis=1)
    early_at = run_ids * half_rows + local_rows
    late_at = (2 * slot_count - 1 - run_ids) * half_rows + local_rows - half_rows
    return jnp.where(local_rows < half_rows, early_at, late_at)


def attend_update(carried, query_block, query_pos, key_block, value_block, key_pos):
    out_sum, run_max, run_total = carried
    scaling = query_block.shape[-1] ** (-0.5)
    scores = (
        jnp.einsum("qhgd,khd->qhgk", query_block, key_block, preferred_element_type=jnp.float32)
        * scaling
    )
    visible = (key_pos[None, :] <= query_pos[:, None])[:, None, None, :]
    scores = jnp.where(visible, scores, mask_floor)
    new_max = jnp.maximum(run_max, jnp.max(scores, axis=-1))
    weights = jnp.where(visible, jnp.exp(scores - new_max[..., None]), 0.0)
    factor = jnp.exp(run_max - new_max)
    new_total = run_total * factor + jnp.sum(weights, axis=-1)
    update = jnp.einsum(
        "qhgk,khd->qhgd",
        weights.astype(jnp.bfloat16),
        value_block,
        preferred_element_type=jnp.float32,
    )
    return (out_sum * factor[..., None] + update, new_max, new_total)


def per_device(queries, keys, values, run_index):
    head_q, head_k, head_v = (
        lax.all_to_all(queries, "heads", split_axis=2, concat_axis=0, tiled=True),
        lax.all_to_all(keys, "heads", split_axis=2, concat_axis=0, tiled=True),
        lax.all_to_all(values, "heads", split_axis=2, concat_axis=0, tiled=True),
    )
    splits, piece_rows, q_local, head_width = head_q.shape
    kv_local = head_k.shape[2]
    group_size = q_local // kv_local
    row_count = splits * piece_rows
    half_rows = row_count // 2
    team_size = lax.axis_size("team")
    block_count = lax.axis_size("blk")
    team_at = lax.axis_index("team")
    block_at = lax.axis_index("blk")
    inverse = inverse_freqs(head_width)
    local_rows = jnp.arange(row_count, dtype=jnp.int32)
    own_slot = jnp.zeros((row_count,), jnp.int32) + team_at * block_count + block_at
    own_pos = slot_positions(run_index, own_slot, local_rows, half_rows)
    rot_q = rotate_heads(
        head_q.reshape(row_count, q_local, head_width).astype(jnp.float32), own_pos, inverse
    ).astype(jnp.bfloat16)
    rot_k = rotate_heads(
        head_k.reshape(row_count, kv_local, head_width).astype(jnp.float32), own_pos, inverse
    ).astype(jnp.bfloat16)
    local_v = head_v.reshape(row_count, kv_local, head_width)
    shared_q = lax.all_gather(rot_q, "team", axis=0, tiled=True)
    gathered_rows = jnp.arange(team_size * row_count, dtype=jnp.int32)
    query_slot = gathered_rows // row_count * block_count + block_at
    query_pos = slot_positions(run_index, query_slot, gathered_rows % row_count, half_rows).reshape(
        team_size, 2, half_rows
    )
    split_q = shared_q.reshape(team_size, 2, half_rows, kv_local, group_size, head_width)
    count_q = team_size * half_rows
    early_q = split_q[:, 0].reshape(count_q, kv_local, group_size, head_width)
    late_q = split_q[:, 1].reshape(count_q, kv_local, group_size, head_width)
    early_pos = query_pos[:, 0].reshape(count_q)
    late_pos = query_pos[:, 1].reshape(count_q)

    def empty_state():
        return (
            jnp.zeros((count_q, kv_local, group_size, head_width), jnp.float32),
            jnp.full((count_q, kv_local, group_size), mask_floor, jnp.float32),
            jnp.zeros((count_q, kv_local, group_size), jnp.float32),
        )

    key_piece = lax.all_gather(rot_k, "blk", axis=0, tiled=True)
    value_piece = lax.all_gather(local_v, "blk", axis=0, tiled=True)
    piece_count = key_piece.shape[0]
    shard_count = piece_count // row_count
    per_step = math.gcd(shard_count, max(1, 1536 // row_count))
    step_count = shard_count // per_step
    key_rows = jnp.arange(piece_count, dtype=jnp.int32)
    key_slot = team_at * block_count + key_rows // row_count
    key_pos = slot_positions(run_index, key_slot, key_rows % row_count, half_rows)
    key_steps = key_piece.reshape(step_count, per_step, row_count, kv_local, head_width)
    value_steps = value_piece.reshape(step_count, per_step, row_count, kv_local, head_width)
    pos_steps = key_pos.reshape(step_count, per_step, row_count)

    def one_step(carried, inputs):
        early_state, late_state = carried
        key_block, value_block, pos_block = inputs
        early_state = attend_update(
            early_state,
            early_q,
            early_pos,
            key_block[:, :half_rows].reshape(per_step * half_rows, kv_local, head_width),
            value_block[:, :half_rows].reshape(per_step * half_rows, kv_local, head_width),
            pos_block[:, :half_rows].reshape(per_step * half_rows),
        )
        late_state = attend_update(
            late_state,
            late_q,
            late_pos,
            key_block.reshape(per_step * row_count, kv_local, head_width),
            value_block.reshape(per_step * row_count, kv_local, head_width),
            pos_block.reshape(per_step * row_count),
        )
        return ((early_state, late_state), None)

    result, unused = lax.scan(
        one_step, (empty_state(), empty_state()), (key_steps, value_steps, pos_steps)
    )
    early_state, late_state = result

    def joined(early_part, late_part):
        trailing = early_part.shape[1:]
        stacked = jnp.concatenate(
            [
                early_part.reshape((team_size, half_rows) + trailing),
                late_part.reshape((team_size, half_rows) + trailing),
            ],
            axis=1,
        )
        return stacked.reshape((team_size, row_count, q_local) + early_part.shape[3:])

    out_sum = joined(early_state[0], late_state[0])
    run_max = joined(early_state[1], late_state[1])
    run_total = joined(early_state[2], late_state[2])
    sums_in = lax.all_to_all(out_sum, "team", split_axis=0, concat_axis=0, tiled=True)
    maxima = lax.all_to_all(run_max, "team", split_axis=0, concat_axis=0, tiled=True)
    totals_in = lax.all_to_all(run_total, "team", split_axis=0, concat_axis=0, tiled=True)
    highest = jnp.max(maxima, axis=0)
    scale_by = jnp.exp(maxima - highest[None])
    merged = jnp.sum(sums_in * scale_by[..., None], axis=0)
    denominator = jnp.sum(totals_in * scale_by, axis=0)
    return (merged / denominator[..., None]).astype(jnp.bfloat16)


def solution(mesh):
    in_specs = (
        P("heads", ("team", "blk"), None, None),
        P("heads", ("team", "blk"), None, None),
        P("heads", ("team", "blk"), None, None),
        P(),
    )
    out_specs = P(("team", "blk"), "heads", None)
    return jax.shard_map(
        per_device, mesh=mesh, in_specs=in_specs, out_specs=out_specs, check_vma=False
    )
```

profile of v0, /device:TPU:0, one launch (start us, length us, event | category | flops | bytes accessed | tf_op | source)
XLA Modules:
  0.0 114.2 jit_solution(669456576231495554)
XLA Ops:
  0.0 1.5 %copy.42 = bf16[1,32,8,128]{3,1,0,2:T(8,128)(2,1)} copy(bf16[1,32,8,128]{3,2,1,0:T(8,128)(2,1)} %param.5) | data formatting | bytes 131072 | tf_op args[1]
  1.5 4.2 %all-to-all-start = ((bf16[1,32,8,128]{3,1,0,2:T(8,128)(2,1)}), bf16[1,32,8,128]{3,1,0,2:T(8,128)(2,1)S(1)}, u32[]{:S(2)}, u32[]{:S(2)}) async-start(bf16[1,32,8,128]{3,1,0,2:T(8,128)(2,1)} %copy.42), calls=%async_computation | async-start | bytes 131072 | tf_op jit(solution)/shard_map/all_to_all | solution.py:74
  5.8 0.7 select_reduce_fusion.2
  6.5 0.7 select_reduce_fusion.1
  7.3 0.7 select_reduce_fusion
  8.9 1.5 %copy.48 = bf16[1,32,8,128]{3,1,0,2:T(8,128)(2,1)} copy(bf16[1,32,8,128]{3,2,1,0:T(8,128)(2,1)} %param.6) | data formatting | bytes 131072 | tf_op args[2]
  10.4 3.3 %all-to-all-start.2 = ((bf16[1,32,8,128]{3,1,0,2:T(8,128)(2,1)}), bf16[1,32,8,128]{3,1,0,2:T(8,128)(2,1)S(1)}, u32[]{:S(2)}, u32[]{:S(2)}) async-start(bf16[1,32,8,128]{3,1,0,2:T(8,128)(2,1)} %copy.48), calls=%async_computation.2 | async-start | bytes 131072 | tf_op jit(solution)/shard_map/all_to_all | solution.py:75
  13.8 1.8 %copy.44 = bf16[1,32,32,128]{3,1,0,2:T(8,128)(2,1)} copy(bf16[1,32,32,128]{3,2,1,0:T(8,128)(2,1)} %param.4) | data formatting | bytes 524288 | tf_op args[0]
  15.6 2.3 %all-to-all-done.2 = bf16[1,32,8,128]{3,1,0,2:T(8,128)(2,1)S(1)} async-done(((bf16[1,32,8,128]{3,1,0,2:T(8,128)(2,1)}), bf16[1,32,8,128]{3,1,0,2:T(8,128)(2,1)S(1)}, u32[]{:S(2)}, u32[]{:S(2)}) %all-to-all-start.2) | async-done | bytes 65568 | tf_op jit(solution)/shard_map/all_to_all | solution.py:75
  17.8 3.4 %all-to-all-start.1 = ((bf16[1,32,32,128]{3,1,0,2:T(8,128)(2,1)}), bf16[1,32,32,128]{3,1,0,2:T(8,128)(2,1)S(1)}, u32[]{:S(2)}, u32[]{:S(2)}) async-start(bf16[1,32,32,128]{3,1,0,2:T(8,128)(2,1)} %copy.44), calls=%async_computation.1 | async-start | bytes 524288 | tf_op jit(solution)/shard_map/all_to_all | solution.py:73
  21.3 32.4 %all_gather.11 = bf16[512,4,128]{2,0,1:T(8,128)(2,1)S(1)} all-gather(bf16[64,4,128]{2,0,1:T(8,128)(2,1)S(1)} %bitcast.103), channel_id=1, replica_groups=mesh['heads'=2,'team'=2,'blk'=8] {'blk'}, dimensions={0}, use_global_device_ids=true | all-gather | bytes 589824 | tf_op jit(solution)/shard_map/all_gather | solution.py:118
  53.8 0.7 copy-done.1
  54.6 31.3 %all_gather.9 = bf16[512,4,128]{2,0,1:T(8,128)(2,1)S(1)} all-gather(bf16[64,4,128]{2,0,1:T(8,128)(2,1)S(1)} %pad_maximum_fusion.2), channel_id=1, replica_groups=mesh['heads'=2,'team'=2,'blk'=8] {'blk'}, dimensions={0}, use_global_device_ids=true | all-gather | bytes 589824 | tf_op jit(solution)/shard_map/all_gather | solution.py:117
  85.8 0.8 copy-done
  87.3 2.2 %all_gather.10 = bf16[128,16,128]{2,1,0:T(8,128)(2,1)S(1)} all-gather(bf16[64,16,128]{2,1,0:T(8,128)(2,1)S(1)} %pad_maximum_fusion.1), channel_id=1, replica_groups=mesh['heads'=2,'team'=2,'blk'=8] {'team'}, dimensions={0}, use_global_device_ids=true | all-gather | bytes 786432 | tf_op jit(solution)/shard_map/all_gather | solution.py:97
  89.6 0.7 fusion.38
  90.4 0.4 fusion.39
  90.9 0.4 fusion.12
  91.4 1.6 %fusion = (f32[64,4,4]{0,2,1:T(4,128)S(1)}, f32[4,512,64,4]{1,2,3,0:T(8,128)S(1)}) fusion(pred[64,512]{1,0:T(8,128)(4,1)S(1)} %broadcast_compare_fusion, bf16[64,4,4,128]{3,0,2,1:T(8,128)(2,1)} %bitcast.99, bf16[512,4,128]{2,0,1:T(8,128)(2,1)} %copy-done), kind=kOutput, calls=%fused_computation.2 | convolution fusion | flops 135789568 | bytes 2920448 | tf_op jit(solution)/shard_map/while/body/eval_jaxpr/qhgd,khd->qhgk/dot_general | solution.py:53
  93.1 0.7 fusion.1
  93.8 0.3 copy-done.2
  94.2 1.2 %fusion.5 = f32[64,4,4,128]{3,0,2,1:T(8,128)S(1)} fusion(f32[4,512,64,4]{1,2,3,0:T(8,128)S(1)} %get-tuple-element.69, f32[64,4,4]{0,2,1:T(4,128)S(1)} %get-tuple-element.60, pred[64,512]{1,0:T(8,128)(4,1)S(1)} %broadcast_compare_fusion, bf16[512,4,128]{2,0,1:T(8,128)(2,1)S(1)} %copy-done.2, f32[64,4,4]{0,2,1:T(4,128)S(1)} %get-tuple-element.58), kind=kOutput, calls=%fused_computation.9 | convolution fusion | flops 136970240 | bytes 3186688 | tf_op jit(solution)/shard_map/while/body/eval_jaxpr/qhgk,khd->qhgd/dot_general | solution.py:62
  95.3 0.6 fusion.6
  96.0 1.1 copy.61
  97.6 3.7 %all_to_all.48 = f32[2,1,1024]{2,1,0:T(1,128)S(1)} all-to-all(f32[2,1,1024]{2,1,0:T(1,128)S(1)} %reshape.326), channel_id=1, replica_groups=mesh['heads'=2,'team'=2,'blk'=8] {'team'}, dimensions={0} | all-to-all | bytes 16384 | tf_op jit(solution)/shard_map/all_to_all | solution.py:172
  101.3 0.5 broadcast.467
  101.8 0.7 reduce.9
  102.6 3.7 %all_to_all.49 = f32[2,1,1024]{2,1,0:T(1,128)S(1)} all-to-all(f32[2,1,1024]{2,1,0:T(1,128)S(1)} %reshape.324), channel_id=1, replica_groups=mesh['heads'=2,'team'=2,'blk'=8] {'team'}, dimensions={0} | all-to-all | bytes 16384 | tf_op jit(solution)/shard_map/all_to_all | solution.py:171
  106.3 0.7 reduce.8
  107.0 3.6 %all-to-all-start.3 = ((f32[2,64,16,128]{3,1,2,0:T(8,128)}), f32[2,64,16,128]{3,1,2,0:T(8,128)S(1)}, u32[]{:S(2)}, u32[]{:S(2)}) async-start(f32[2,64,16,128]{3,1,2,0:T(8,128)} %copy.61), calls=%async_computation.3 | async-start | bytes 2097152 | tf_op jit(solution)/shard_map/all_to_all | solution.py:170
  110.6 2.1 %all-to-all-done.3 = f32[2,64,16,128]{3,1,2,0:T(8,128)S(1)} async-done(((f32[2,64,16,128]{3,1,2,0:T(8,128)}), f32[2,64,16,128]{3,1,2,0:T(8,128)S(1)}, u32[]{:S(2)}, u32[]{:S(2)}) %all-to-all-start.3) | async-done | bytes 1048608 | tf_op jit(solution)/shard_map/all_to_all | solution.py:170
  113.3 0.9 copy.56
  (57 shorter events, 3.6 us)
Async XLA Ops:
  1.5 8.9 %all-to-all-start = ((bf16[1,32,8,128]{3,1,0,2:T(8,128)(2,1)}), bf16[1,32,8,128]{3,1,0,2:T(8,128)(2,1)S(1)}, u32[]{:S(2)}, u32[]{:S(2)}) async-start(bf16[1,32,8,128]{3,1,0,2:T(8,128)(2,1)} %copy.42), calls=%async_computation | async-start | bytes 131072 | tf_op jit(solution)/shard_map/all_to_all | solution.py:74
  10.4 7.4 %all-to-all-start.2 = ((bf16[1,32,8,128]{3,1,0,2:T(8,128)(2,1)}), bf16[1,32,8,128]{3,1,0,2:T(8,128)(2,1)S(1)}, u32[]{:S(2)}, u32[]{:S(2)}) async-start(bf16[1,32,8,128]{3,1,0,2:T(8,128)(2,1)} %copy.48), calls=%async_computation.2 | async-start | bytes 131072 | tf_op jit(solution)/shard_map/all_to_all | solution.py:75
  17.8 68.8 %all-to-all-start.1 = ((bf16[1,32,32,128]{3,1,0,2:T(8,128)(2,1)}), bf16[1,32,32,128]{3,1,0,2:T(8,128)(2,1)S(1)}, u32[]{:S(2)}, u32[]{:S(2)}) async-start(bf16[1,32,32,128]{3,1,0,2:T(8,128)(2,1)} %copy.44), calls=%async_computation.1 | async-start | bytes 524288 | tf_op jit(solution)/shard_map/all_to_all | solution.py:73
  53.7 0.8 copy-start.1
  85.8 0.8 copy-start
  93.1 1.0 copy-start.2
  107.0 5.7 %all-to-all-start.3 = ((f32[2,64,16,128]{3,1,2,0:T(8,128)}), f32[2,64,16,128]{3,1,2,0:T(8,128)S(1)}, u32[]{:S(2)}, u32[]{:S(2)}) async-start(f32[2,64,16,128]{3,1,2,0:T(8,128)} %copy.61), calls=%async_computation.3 | async-start | bytes 2097152 | tf_op jit(solution)/shard_map/all_to_all | solution.py:170
where the time goes:
time: 115 us; the launch traced here: 114 us
  blocking collectives  73.2 us (64%)
  starting transfers between devices  14.5 us (13%)
  local copies, waits for them, and re-layouts  11.3 us (10%)
  other arithmetic  6.65 us (6%)
  waiting for transfers between devices  4.35 us (4%)
  matrix products  3.81 us (3%)
    all_gather x1, blocking collectives, per_device(): value_piece = lax.all_gather(local_v, 'blk', axis=0, tiled=True)  32.4 us
    all_gather x1, blocking collectives, per_device(): key_piece = lax.all_gather(rot_k, 'blk', axis=0, tiled=True)  31.3 us
    unnamed x13, local copies, waits for them, and re-layouts  6.84 us
    all_to_all x1, starting transfers between devices, per_device(): lax.all_to_all(keys, 'heads', split_axis=2, concat_axis=0, tiled=True)  4.21 us
    all_to_all x1, blocking collectives, per_device(): lax.all_to_all(run_max, 'team', split_axis=0, concat_axis=0, tiled=True)  3.7 us
    all_to_all x1, blocking collectives, per_device(): lax.all_to_all(run_total, 'team', split_axis=0, concat_axis=0, tiled=True)  3.7 us
    all_to_all x1, starting transfers between devices, per_device(): lax.all_to_all(out_sum, 'team', split_axis=0, concat_axis=0, tiled=True)  3.58 us
    all_to_all x1, starting transfers between devices, per_device(): lax.all_to_all(queries, 'heads', split_axis=2, concat_axis=0, tiled=True)  3.44 us
  transfers between devices with their start and end apart: 4, of which 2 were waited for; matrix products, arithmetic and copies ran while one was open for 6% of the time, Pallas kernels for 0%

commit v1 on v0

v1 whole, which is shorter than its diff:
```python
import functools
import math

import jax
import jax.numpy as jnp
import numpy as np
from jax import lax
from jax.experimental import pallas as pl
from jax.experimental.pallas import tpu as pltpu
from jax.sharding import PartitionSpec as P

mask_floor = -1e30
rope_theta = 500000.0
rope_factor = 8.0
low_factor = 1.0
high_factor = 4.0
initial_context = 8192.0


def inverse_freqs(head_width):
    counter = np.arange(head_width // 2, dtype=np.float64)
    base_freq = 1.0 / rope_theta ** (2.0 * counter / head_width)
    wavelength = 2.0 * np.pi / base_freq
    smooth = (initial_context / wavelength - low_factor) / (high_factor - low_factor)
    blended = (1.0 - smooth) * base_freq / rope_factor + smooth * base_freq
    middle = np.where(wavelength > initial_context / low_factor, base_freq / rope_factor, blended)
    return np.where(wavelength < initial_context / high_factor, base_freq, middle)


def small_loop(first, last, body):
    if last - first <= 4:
        for at in range(first, last):
            body(at)
    else:
        lax.fori_loop(first, last, lambda at, unused: (body(at), unused)[1], 0)


def attend_kernel(
    dims,
    run_ref,
    freq_ref,
    q_ref,
    k_ref,
    v_ref,
    out_ref,
    kv_out,
    q_out,
    kv_all,
    q_all,
    acc_ref,
    max_ref,
    sum_ref,
    out_part,
    kv_send,
    kv_recv,
    q_send,
    q_recv,
    z_send,
    z_recv,
    y_send,
    y_recv,
    o_send,
    o_recv,
):
    X, C, Z, Y, R, KVL, G, D = dims
    S = C * Z * Y
    half = X * R // 2
    rows = C * G * R
    x, c, b = lax.axis_index("heads"), lax.axis_index("team"), lax.axis_index("blk")
    z, y = b // Y, b % Y
    mine = x * C + c
    power_of_two = Z & (Z - 1) == 0

    def z_to(k):
        if power_of_two and isinstance(k, int):
            at, bit = 0, 1
            while bit < Z:
                at = at + (z // bit + k // bit) % 2 * bit
                bit *= 2
            return at
        return (z + k) % Z

    def z_from(k):
        if power_of_two and isinstance(k, int):
            return z_to(k)
        return (z + Z - k) % Z

    def y_to(m):
        return (y + m) % Y

    def y_from(m):
        return (y + Y - m) % Y

    def device(xx, cc, bb):
        return {"heads": xx, "team": cc, "blk": bb}

    offsets = [(dx, dc) for dx in range(X) for dc in range(C) if (dx, dc) != (0, 0)]

    barrier = pltpu.get_barrier_semaphore()

    def greet(xx, cc, bb):
        pl.semaphore_signal(
            barrier, inc=1, device_id=device(xx, cc, bb), device_id_type=pl.DeviceIdType.MESH
        )

    for dx, dc in offsets:
        greet((x + dx) % X, (c + dc) % C, b)
    small_loop(1, Z, lambda k: greet(x, c, z_to(k) * Y + y))
    small_loop(1, Y, lambda m: greet(x, c, z * Y + y_to(m)))

    def first_pos(slot, piece):
        run = run_ref[slot]
        start = piece * R
        if isinstance(piece, int):
            return run * half + start if start < half else (2 * S - 1 - run) * half + start - half
        return jnp.where(start < half, run * half, (2 * S - 1 - run) * half - half) + start

    own_first = first_pos(c * (Z * Y) + b, x)
    pos = own_first + lax.broadcasted_iota(jnp.int32, (R, D), 0)
    angles = pos.astype(jnp.float32) * freq_ref[...]
    cosine = jnp.cos(angles)
    sine = jnp.sin(angles)
    lanes = lax.broadcasted_iota(jnp.int32, (R, D), 1)
    sine = jnp.where(lanes < D // 2, -sine, sine)

    def by_head(ref, first, count):
        return jnp.swapaxes(ref[0, :, first : first + count, :].astype(jnp.float32), 0, 1)

    def rotated(values):
        turned = pltpu.roll(values, D // 2, 2)
        return values * cosine[None] + turned * sine[None]

    kv_heads = X * C * KVL
    kv_out[:, 0] = (
        rotated(by_head(k_ref, 0, kv_heads)).astype(jnp.bfloat16).reshape(X * C, KVL, R, D)
    )
    kv_out[:, 1] = by_head(v_ref, 0, kv_heads).astype(jnp.bfloat16).reshape(X * C, KVL, R, D)
    kv_all[0, 0, x, :, :, c] = kv_out[mine]

    pl.semaphore_wait(barrier, len(offsets) + Z - 1 + Y - 1)

    def remote(src, dst, send, recv, to):
        return pltpu.make_async_remote_copy(
            src_ref=src,
            dst_ref=dst,
            send_sem=send,
            recv_sem=recv,
            device_id=to,
            device_id_type=pl.DeviceIdType.MESH,
        )

    def kv_copy(dx, dc):
        xx, cc = (x + dx) % X, (c + dc) % C
        return remote(
            kv_out.at[xx * C + cc],
            kv_all.at[0, 0, x, :, :, c],
            kv_send.at[dx, dc],
            kv_recv.at[dx, dc],
            device(xx, cc, b),
        )

    def q_copy(dx, dc):
        xx, cc = (x + dx) % X, (c + dc) % C
        return remote(
            q_out.at[xx * C + cc],
            q_all.at[x, :, c],
            q_send.at[dx, dc],
            q_recv.at[dx, dc],
            device(xx, cc, b),
        )

    for dx, dc in offsets:
        kv_copy(dx, dc).start()

    q_heads = KVL * G
    for to in range(X * C):
        q_out[to] = (
            rotated(by_head(q_ref, to * q_heads, q_heads))
            .astype(jnp.bfloat16)
            .reshape(KVL, G, R, D)
        )
    q_all[x, :, c] = q_out[mine]
    for dx, dc in offsets:
        q_copy(dx, dc).start()

    def z_copy(k, piece):
        return remote(
            kv_all.at[0, 0, piece],
            kv_all.at[k, 0, piece],
            z_send.at[k, piece],
            z_recv.at[k, piece],
            device(x, c, z_to(k) * Y + y),
        )

    def y_copy(k, m, piece):
        return remote(
            kv_all.at[k, 0, piece],
            kv_all.at[k, m, piece],
            y_send.at[k, m, piece],
            y_recv.at[k, m, piece],
            device(x, c, z * Y + y_to(m)),
        )

    def piece_at(dx):
        return (x + X - dx) % X

    for dx in range(X):
        for dc in range(C):
            if (dx, dc) != (0, 0):
                kv_copy(dx, dc).wait_recv()
        piece = piece_at(dx)
        small_loop(1, Z, lambda k: z_copy(k, piece).start())
        small_loop(1, Y, lambda m: y_copy(0, m, piece).start())

    def pass_on(k):
        for dx in range(X):
            piece = piece_at(dx)
            z_copy(k, piece).wait_recv()
            small_loop(1, Y, lambda m: y_copy(k, m, piece).start())

    scaling = math.log2(math.e) * D ** (-0.5)

    def key_positions(k, pieces):
        count = len(pieces) * Y * C * R
        lane = lax.broadcasted_iota(jnp.int32, (1, count), 1)
        segment = lane // R
        total = lane % R
        at = 0
        for piece in pieces:
            for m in range(Y):
                for t in range(C):
                    slot = t * (Z * Y) + z_from(k) * Y + y_from(m)
                    total = total + jnp.where(segment == at, first_pos(slot, piece), 0)
                    at += 1
        return total

    def query_positions(piece):
        row = lax.broadcasted_iota(jnp.int32, (rows, 1), 0)
        total = row % R
        for t in range(C):
            total = total + jnp.where(row // (G * R) == t, first_pos(t * (Z * Y) + b, piece), 0)
        return total

    early = list(range(X // 2))
    late = list(range(X // 2, X))

    def attend(k, first):
        def units(kind, head, pieces):
            return jnp.concatenate(
                [kv_all[k, m, p, kind, head].reshape(C * R, D) for p in pieces for m in range(Y)],
                axis=0,
            )

        key_pos = {"early": key_positions(k, early), "late": key_positions(k, late)}
        for head in range(KVL):
            keys = {"early": units(0, head, early), "late": units(0, head, late)}
            values = {"early": units(1, head, early), "late": units(1, head, late)}
            for piece in range(X):
                query = q_all[piece, head].reshape(rows, D)
                query_pos = query_positions(piece)
                own = "early" if piece in early else "late"
                parts = ["early"] if own == "early" else ["early", "late"]
                scores = []
                for part in parts:
                    s = lax.dot_general(
                        query, keys[part], (((1,), (1,)), ((), ())),
                        preferred_element_type=jnp.float32,
                    )
                    if part == own:
                        s = jnp.where(key_pos[part] <= query_pos, s, mask_floor)
                    scores.append(s)
                top = functools.reduce(
                    jnp.maximum, [jnp.max(s, axis=-1, keepdims=True) for s in scores]
                )
                if not first:
                    before = max_ref[piece, head]
                    top = jnp.maximum(top, before)
                    factor = jnp.exp2((before - top) * scaling)
                weights = [jnp.exp2((s - top) * scaling) for s in scores]
                total = sum(jnp.sum(w, axis=-1, keepdims=True) for w in weights)
                update = sum(
                    jnp.dot(
                        w.astype(jnp.bfloat16), values[part], preferred_element_type=jnp.float32
                    )
                    for w, part in zip(weights, parts)
                )
                if not first:
                    total = total + sum_ref[piece, head] * factor
                    update = update + acc_ref[piece, head] * factor
                max_ref[piece, head] = top
                sum_ref[piece, head] = total
                acc_ref[piece, head] = update


    if Z > 1:
        pass_on(1)
    for dx, dc in offsets:
        q_copy(dx, dc).wait_recv()

    def arrive(k):
        for dx in range(X):
            piece = piece_at(dx)
            small_loop(1, Y, lambda m: y_copy(k, m, piece).wait_recv())

    arrive(0)
    attend(0, True)

    def later(k):
        if isinstance(k, int):
            if k + 1 < Z:
                pass_on(k + 1)
        else:
            pl.when(k + 1 < Z)(lambda: pass_on(k + 1))
        arrive(k)
        attend(k, False)

    small_loop(1, Z, later)

    def o_copy(dc, piece):
        cc = (c + dc) % C
        return remote(
            out_part.at[piece, cc],
            out_ref.at[c, :, :, pl.ds(piece * R, R)],
            o_send.at[dc, piece],
            o_recv.at[dc, piece],
            device(x, cc, b),
        )

    for piece in range(X):
        for head in range(KVL):
            mixed = acc_ref[piece, head] / sum_ref[piece, head]
            out_part[piece, :, head] = mixed.astype(jnp.bfloat16).reshape(C, G, R, D)
        for dc in range(1, C):
            o_copy(dc, piece).start()
        out_ref[c, :, :, pl.ds(piece * R, R)] = out_part[piece, c]

    for dx, dc in offsets:
        kv_copy(dx, dc).wait_send()
        q_copy(dx, dc).wait_send()
    for piece in range(X):
        small_loop(1, Z, lambda k: z_copy(k, piece).wait_send())

        def sent(k):
            small_loop(1, Y, lambda m: y_copy(k, m, piece).wait_send())

        small_loop(0, Z, sent)
    for piece in range(X):
        for dc in range(1, C):
            o_copy(dc, piece).wait()


def per_device(queries, keys, values, run_index):
    X, C, B = lax.axis_size("heads"), lax.axis_size("team"), lax.axis_size("blk")
    R, QH, D = queries.shape[1:]
    KVH = keys.shape[2]
    KVL = KVH // (X * C)
    G = QH // KVH
    Y = max(d for d in range(1, math.isqrt(B) + 1) if B % d == 0)
    Z = B // Y
    freqs = inverse_freqs(D)
    freqs = jnp.asarray(np.concatenate([freqs, freqs])[None], jnp.float32)
    rows = C * G * R
    vmem = pl.BlockSpec(memory_space=pltpu.VMEM)
    dma = pltpu.SemaphoreType.DMA
    bf16, f32 = jnp.bfloat16, jnp.float32
    out = pl.pallas_call(
        functools.partial(attend_kernel, (X, C, Z, Y, R, KVL, G, D)),
        out_shape=jax.ShapeDtypeStruct((C, KVL, G, X * R, D), bf16),
        in_specs=[pl.BlockSpec(memory_space=pltpu.SMEM)] + [vmem] * 4,
        out_specs=vmem,
        scratch_shapes=[
            pltpu.VMEM((X * C, 2, KVL, R, D), bf16),
            pltpu.VMEM((X * C, KVL, G, R, D), bf16),
            pltpu.VMEM((Z, Y, X, 2, KVL, C, R, D), bf16),
            pltpu.VMEM((X, KVL, C, G, R, D), bf16),
            pltpu.VMEM((X, KVL, rows, D), f32),
            pltpu.VMEM((X, KVL, rows, 1), f32),
            pltpu.VMEM((X, KVL, rows, 1), f32),
            pltpu.VMEM((X, C, KVL, G, R, D), bf16),
            dma((X, C)),
            dma((X, C)),
            dma((X, C)),
            dma((X, C)),
            dma((Z, X)),
            dma((Z, X)),
            dma((Z, Y, X)),
            dma((Z, Y, X)),
            dma((C, X)),
            dma((C, X)),
        ],
        compiler_params=pltpu.CompilerParams(
            collective_id=0, has_side_effects=True, vmem_limit_bytes=48 * 2**20
        ),
    )(run_index, freqs, queries, keys, values)
    return jnp.transpose(out.reshape(C * KVL * G, X * R, D), (1, 0, 2))


def solution(mesh):
    in_specs = (
        P("heads", ("team", "blk"), None, None),
        P("heads", ("team", "blk"), None, None),
        P("heads", ("team", "blk"), None, None),
        P(),
    )
    out_specs = P(("team", "blk"), "heads", None)
    return jax.shard_map(
        per_device, mesh=mesh, in_specs=in_specs, out_specs=out_specs, check_vma=False
    )
```

time: 115 us -> 33 us (0.29)
  blocking collectives: 73.2 us -> 0 us
  Pallas kernels: 0 us -> 27.9 us
  starting transfers between devices: 14.5 us -> 0 us
  other arithmetic: 6.65 us -> 0 us
  local copies, waits for them, and re-layouts: 11.3 us -> 4.81 us
  waiting for transfers between devices: 4.35 us -> 0 us
  matrix products: 3.81 us -> 0 us
    all_gather x3 -> x0, blocking collectives: 65.8 us -> none  [the longest x1 32.4 us: per_device(): value_piece = lax.all_gather(local_v, 'blk', axis=0, tiled=True)]
    pallas_call x0 -> x1, Pallas kernels: none -> 27.9 us  [per_device(): pl.pallas_call(functools.partial(attend_kernel, (X, C, Z, Y, R, KVL, G, D...]
    all_to_all x4 -> x0, starting transfers between devices: 14.5 us -> none  [the longest x1 4.21 us: per_device(): lax.all_to_all(keys, 'heads', split_axis=2, concat_axis=0, tiled=True)]
    all_to_all x2 -> x0, blocking collectives: 7.4 us -> none  [the longest x1 3.7 us: per_device(): lax.all_to_all(run_max, 'team', split_axis=0, concat_axis=0, tiled=True)]
    all_to_all x4 -> x0, waiting for transfers between devices: 4.35 us -> none  [the longest x1 2.27 us: per_device(): lax.all_to_all(values, 'heads', split_axis=2, concat_axis=0, tiled=True)]
    dot_general x4 -> x0, matrix products: 3.81 us -> none  [the longest x2 2.03 us: attend_update(): jnp.einsum('qhgd,khd->qhgk', query_block, key_block, preferred_element_ty...]
    reduce_sum x7 -> x0, other arithmetic: 3.7 us -> none  [the longest x3 2.23 us: slot_positions(): run_ids = jnp.sum(jnp.where(matches, run_index[None, :], 0), axis=1)]
    unnamed x13 -> x10, local copies, waits for them, and re-layouts: 6.84 us -> 3.94 us
  transfers between devices with their start and end apart: 4 -> 0, of which waited for: 2 -> 0; matrix products, arithmetic and copies ran while one was open for 6% -> 0% of each run, Pallas kernels for 0% -> 0%
where the time goes in v1:
time: 33 us; the launch traced here: 32.8 us
  Pallas kernels  27.9 us (85%)
  local copies, waits for them, and re-layouts  4.81 us (15%)
    pallas_call x1, Pallas kernels, per_device(): pl.pallas_call(functools.partial(attend_kernel, (X, C, Z, Y, R, KVL, G, D...  27.9 us
    unnamed x10, local copies, waits for them, and re-layouts  3.94 us
    reshape x1, local copies, waits for them, and re-layouts, per_device(): return jnp.transpose(out.reshape(C * KVL * G, X * R, D), (1, 0, 2))  0.88 us

profile of v1, /device:TPU:0, one launch (start us, length us, event | category | flops | bytes accessed | tf_op | source)
XLA Modules:
  0.0 32.8 jit_solution(147881477263018944)
XLA Ops:
  0.0 0.0 copy-start
  0.0 0.9 %copy-done = bf16[1,32,32,128]{3,2,1,0:T(8,128)(2,1)S(1)} copy-done((bf16[1,32,32,128]{3,2,1,0:T(8,128)(2,1)S(1)}, bf16[1,32,32,128]{3,2,1,0:T(8,128)(2,1)}, u32[]{:S(2)}) %copy-start) | copy-done | bytes 262168
  1.0 0.0 copy-start.1
  1.0 0.8 %copy-done.1 = bf16[1,32,8,128]{3,2,1,0:T(8,128)(2,1)S(1)} copy-done((bf16[1,32,8,128]{3,2,1,0:T(8,128)(2,1)S(1)}, bf16[1,32,8,128]{3,2,1,0:T(8,128)(2,1)}, u32[]{:S(2)}) %copy-start.1) | copy-done | bytes 65560
  1.8 0.0 copy-start.2
  1.8 0.8 %copy-done.2 = bf16[1,32,8,128]{3,2,1,0:T(8,128)(2,1)S(1)} copy-done((bf16[1,32,8,128]{3,2,1,0:T(8,128)(2,1)S(1)}, bf16[1,32,8,128]{3,2,1,0:T(8,128)(2,1)}, u32[]{:S(2)}) %copy-start.2) | copy-done | bytes 65560
  2.6 0.0 copy-start.3
  2.6 0.7 %copy-done.3 = s32[16]{0:T(128)S(1)} copy-done((s32[16]{0:T(128)S(1)}, s32[16]{0:T(128)}, u32[]{:S(2)}) %copy-start.3) | copy-done | bytes 88
  3.3 0.0 copy-start.4
  3.3 0.7 %copy-done.4 = f32[1,128]{1,0:T(1,128)S(1)} copy-done((f32[1,128]{1,0:T(1,128)S(1)}, f32[1,128]{1,0:T(1,128)}, u32[]{:S(2)}) %copy-start.4) | copy-done | bytes 536
  3.9 27.9 %shard_map.55 = bf16[2,2,4,64,128]{4,3,2,1,0:T(8,128)(2,1)S(1)} custom-call(s32[16]{0:T(128)S(1)} %copy-done.3, f32[1,128]{1,0:T(1,128)S(1)} %copy-done.4, bf16[1,32,32,128]{3,2,1,0:T(8,128)(2,1)S(1)} %copy-done, bf16[1,32,8,128]{3,2,1,0:T(8,128)(2,1)S(1)} %copy-done.1, bf16[1,32,8,128]{3,2,1,0:T(8,128)(2,1)S(1)} %copy-done.2), custom_call_target="tpu_custom_call" | custom-call | tf_op jit(solution)/shard_map/pallas_call | solution.py:366
  31.9 0.9 %copy.8 = bf16[16,64,128]{2,0,1:T(8,128)(2,1)} copy(bf16[16,64,128]{2,1,0:T(8,128)(2,1)S(1)} %bitcast.4) | data formatting | bytes 524288 | tf_op jit(solution)/shard_map/reshape | solution.py:395
Async XLA Ops:
  0.0 0.9 %copy-start = (bf16[1,32,32,128]{3,2,1,0:T(8,128)(2,1)S(1)}, bf16[1,32,32,128]{3,2,1,0:T(8,128)(2,1)}, u32[]{:S(2)}) copy-start(bf16[1,32,32,128]{3,2,1,0:T(8,128)(2,1)} %q_ref.1) | copy-start | bytes 786436
  1.0 0.8 %copy-start.1 = (bf16[1,32,8,128]{3,2,1,0:T(8,128)(2,1)S(1)}, bf16[1,32,8,128]{3,2,1,0:T(8,128)(2,1)}, u32[]{:S(2)}) copy-start(bf16[1,32,8,128]{3,2,1,0:T(8,128)(2,1)} %k_ref.1) | copy-start | bytes 196612
  1.8 0.8 %copy-start.2 = (bf16[1,32,8,128]{3,2,1,0:T(8,128)(2,1)S(1)}, bf16[1,32,8,128]{3,2,1,0:T(8,128)(2,1)}, u32[]{:S(2)}) copy-start(bf16[1,32,8,128]{3,2,1,0:T(8,128)(2,1)} %v_ref.1) | copy-start | bytes 196612
  2.6 0.7 %copy-start.3 = (s32[16]{0:T(128)S(1)}, s32[16]{0:T(128)}, u32[]{:S(2)}) copy-start(s32[16]{0:T(128)} %run_ref.1) | copy-start | bytes 196
  3.3 0.7 %copy-start.4 = (f32[1,128]{1,0:T(1,128)S(1)}, f32[1,128]{1,0:T(1,128)}, u32[]{:S(2)}) copy-start(f32[1,128]{1,0:T(1,128)} %constant.2.clone.freq_ref) | copy-start | bytes 1540

commit v2 on v1

--- a/solution.py
+++ b/solution.py
@@ -37,12 +37,18 @@
 
 def attend_kernel(
     dims,
+    run_hbm,
+    freq_hbm,
+    q_hbm,
+    k_hbm,
+    v_hbm,
+    out_ref,
     run_ref,
     freq_ref,
     q_ref,
     k_ref,
     v_ref,
-    out_ref,
+    load_sem,
     kv_out,
     q_out,
     kv_all,
@@ -69,22 +75,6 @@
     x, c, b = lax.axis_index("heads"), lax.axis_index("team"), lax.axis_index("blk")
     z, y = b // Y, b % Y
     mine = x * C + c
-    power_of_two = Z & (Z - 1) == 0
-
-    def z_to(k):
-        if power_of_two and isinstance(k, int):
-            at, bit = 0, 1
-            while bit < Z:
-                at = at + (z // bit + k // bit) % 2 * bit
-                bit *= 2
-            return at
-        return (z + k) % Z
-
-    def z_from(k):
-        if power_of_two and isinstance(k, int):
-            return z_to(k)
-        return (z + Z - k) % Z
-
     def y_to(m):
         return (y + m) % Y
 
@@ -93,6 +83,25 @@
 
     def device(xx, cc, bb):
         return {"heads": xx, "team": cc, "blk": bb}
+
+    loads = [
+        pltpu.make_async_copy(src, dst, load_sem.at[at])
+        for at, (src, dst) in enumerate(
+            [(run_hbm, run_ref), (freq_hbm, freq_ref), (k_hbm, k_ref), (v_hbm, v_ref), (q_hbm, q_ref)]
+        )
+    ]
+    for load in loads:
+        load.start()
+
+    low, high = z, Z - 1 - z
+    near = jnp.minimum(low, high)
+
+    def z_near(k):
+        if isinstance(k, int) and k == 0:
+            return z
+        paired = jnp.where(k % 2 == 1, z - (k + 1) // 2, z + k // 2)
+        single = jnp.where(low < high, z + (k - near), z - (k - near))
+        return jnp.where(k <= 2 * near, paired, single)
 
     offsets = [(dx, dc) for dx in range(X) for dc in range(C) if (dx, dc) != (0, 0)]
 
@@ -105,7 +114,8 @@
 
     for dx, dc in offsets:
         greet((x + dx) % X, (c + dc) % C, b)
-    small_loop(1, Z, lambda k: greet(x, c, z_to(k) * Y + y))
+    pl.when(z > 0)(lambda: greet(x, c, b - Y))
+    pl.when(z < Z - 1)(lambda: greet(x, c, b + Y))
     small_loop(1, Y, lambda m: greet(x, c, z * Y + y_to(m)))
 
     def first_pos(slot, piece):
@@ -114,6 +124,9 @@
         if isinstance(piece, int):
             return run * half + start if start < half else (2 * S - 1 - run) * half + start - half
         return jnp.where(start < half, run * half, (2 * S - 1 - run) * half - half) + start
+
+    loads[0].wait()
+    loads[1].wait()
 
     own_first = first_pos(c * (Z * Y) + b, x)
     pos = own_first + lax.broadcasted_iota(jnp.int32, (R, D), 0)
@@ -130,14 +143,16 @@
         turned = pltpu.roll(values, D // 2, 2)
         return values * cosine[None] + turned * sine[None]
 
+    loads[2].wait()
+    loads[3].wait()
     kv_heads = X * C * KVL
     kv_out[:, 0] = (
         rotated(by_head(k_ref, 0, kv_heads)).astype(jnp.bfloat16).reshape(X * C, KVL, R, D)
     )
     kv_out[:, 1] = by_head(v_ref, 0, kv_heads).astype(jnp.bfloat16).reshape(X * C, KVL, R, D)
-    kv_all[0, 0, x, :, :, c] = kv_out[mine]
-
-    pl.semaphore_wait(barrier, len(offsets) + Z - 1 + Y - 1)
+    kv_all[z, 0, x, :, :, c] = kv_out[mine]
+
+    pl.semaphore_wait(barrier, len(offsets) + Y - 1 + jnp.minimum(z, 1) + jnp.minimum(Z - 1 - z, 1))
 
     def remote(src, dst, send, recv, to):
         return pltpu.make_async_remote_copy(
@@ -153,7 +168,7 @@
         xx, cc = (x + dx) % X, (c + dc) % C
         return remote(
             kv_out.at[xx * C + cc],
-            kv_all.at[0, 0, x, :, :, c],
+            kv_all.at[z, 0, x, :, :, c],
             kv_send.at[dx, dc],
             kv_recv.at[dx, dc],
             device(xx, cc, b),
@@ -172,6 +187,7 @@
     for dx, dc in offsets:
         kv_copy(dx, dc).start()
 
+    loads[4].wait()
     q_heads = KVL * G
     for to in range(X * C):
         q_out[to] = (
@@ -183,40 +199,43 @@
     for dx, dc in offsets:
         q_copy(dx, dc).start()
 
-    def z_copy(k, piece):
+    def z_copy(at, up, piece):
         return remote(
-            kv_all.at[0, 0, piece],
-            kv_all.at[k, 0, piece],
-            z_send.at[k, piece],
-            z_recv.at[k, piece],
-            device(x, c, z_to(k) * Y + y),
-        )
-
-    def y_copy(k, m, piece):
+            kv_all.at[at, 0, piece],
+            kv_all.at[at, 0, piece],
+            z_send.at[up, at, piece],
+            z_recv.at[at, piece],
+            device(x, c, b + Y if up else b - Y),
+        )
+
+    def y_copy(at, m, piece):
         return remote(
-            kv_all.at[k, 0, piece],
-            kv_all.at[k, m, piece],
-            y_send.at[k, m, piece],
-            y_recv.at[k, m, piece],
+            kv_all.at[at, 0, piece],
+            kv_all.at[at, m, piece],
+            y_send.at[at, m, piece],
+            y_recv.at[at, m, piece],
             device(x, c, z * Y + y_to(m)),
         )
 
     def piece_at(dx):
         return (x + X - dx) % X
+
+    def pass_on(at, piece):
+        pl.when((at <= z) & (z < Z - 1))(lambda: z_copy(at, 1, piece).start())
+        pl.when((at >= z) & (z > 0))(lambda: z_copy(at, 0, piece).start())
+        small_loop(1, Y, lambda m: y_copy(at, m, piece).start())
 
     for dx in range(X):
         for dc in range(C):
             if (dx, dc) != (0, 0):
                 kv_copy(dx, dc).wait_recv()
-        piece = piece_at(dx)
-        small_loop(1, Z, lambda k: z_copy(k, piece).start())
-        small_loop(1, Y, lambda m: y_copy(0, m, piece).start())
-
-    def pass_on(k):
+        pass_on(z, piece_at(dx))
+
+    def receive(k):
+        at = z_near(k)
         for dx in range(X):
-            piece = piece_at(dx)
-            z_copy(k, piece).wait_recv()
-            small_loop(1, Y, lambda m: y_copy(k, m, piece).start())
+            z_copy(at, 1, piece_at(dx)).wait_recv()
+            pass_on(at, piece_at(dx))
 
     scaling = math.log2(math.e) * D ** (-0.5)
 
@@ -229,7 +248,7 @@
         for piece in pieces:
             for m in range(Y):
                 for t in range(C):
-                    slot = t * (Z * Y) + z_from(k) * Y + y_from(m)
+                    slot = t * (Z * Y) + z_near(k) * Y + y_from(m)
                     total = total + jnp.where(segment == at, first_pos(slot, piece), 0)
                     at += 1
         return total
@@ -245,9 +264,11 @@
     late = list(range(X // 2, X))
 
     def attend(k, first):
+        at = z_near(k)
+
         def units(kind, head, pieces):
             return jnp.concatenate(
-                [kv_all[k, m, p, kind, head].reshape(C * R, D) for p in pieces for m in range(Y)],
+                [kv_all[at, m, p, kind, head].reshape(C * R, D) for p in pieces for m in range(Y)],
                 axis=0,
             )
 
@@ -293,14 +314,14 @@
 
 
     if Z > 1:
-        pass_on(1)
+        receive(1)
     for dx, dc in offsets:
         q_copy(dx, dc).wait_recv()
 
     def arrive(k):
         for dx in range(X):
             piece = piece_at(dx)
-            small_loop(1, Y, lambda m: y_copy(k, m, piece).wait_recv())
+            small_loop(1, Y, lambda m: y_copy(z_near(k), m, piece).wait_recv())
 
     arrive(0)
     attend(0, True)
@@ -308,9 +329,9 @@
     def later(k):
         if isinstance(k, int):
             if k + 1 < Z:
-                pass_on(k + 1)
+                receive(k + 1)
         else:
-            pl.when(k + 1 < Z)(lambda: pass_on(k + 1))
+            pl.when(k + 1 < Z)(lambda: receive(k + 1))
         arrive(k)
         attend(k, False)
 
@@ -326,27 +347,34 @@
             device(x, cc, b),
         )
 
+    def own_copy(piece):
+        return pltpu.make_async_copy(
+            out_part.at[piece, c], out_ref.at[c, :, :, pl.ds(piece * R, R)], o_send.at[0, piece]
+        )
+
     for piece in range(X):
         for head in range(KVL):
             mixed = acc_ref[piece, head] / sum_ref[piece, head]
             out_part[piece, :, head] = mixed.astype(jnp.bfloat16).reshape(C, G, R, D)
         for dc in range(1, C):
             o_copy(dc, piece).start()
-        out_ref[c, :, :, pl.ds(piece * R, R)] = out_part[piece, c]
+        own_copy(piece).start()
 
     for dx, dc in offsets:
         kv_copy(dx, dc).wait_send()
         q_copy(dx, dc).wait_send()
     for piece in range(X):
-        small_loop(1, Z, lambda k: z_copy(k, piece).wait_send())
-
-        def sent(k):
-            small_loop(1, Y, lambda m: y_copy(k, m, piece).wait_send())
+
+        def sent(at):
+            pl.when((at <= z) & (z < Z - 1))(lambda: z_copy(at, 1, piece).wait_send())
+            pl.when((at >= z) & (z > 0))(lambda: z_copy(at, 0, piece).wait_send())
+            small_loop(1, Y, lambda m: y_copy(at, m, piece).wait_send())
 
         small_loop(0, Z, sent)
     for piece in range(X):
         for dc in range(1, C):
             o_copy(dc, piece).wait()
+        own_copy(piece).wait()
 
 
 def per_device(queries, keys, values, run_index):
@@ -360,15 +388,21 @@
     freqs = inverse_freqs(D)
     freqs = jnp.asarray(np.concatenate([freqs, freqs])[None], jnp.float32)
     rows = C * G * R
-    vmem = pl.BlockSpec(memory_space=pltpu.VMEM)
+    hbm = pl.BlockSpec(memory_space=pltpu.HBM)
     dma = pltpu.SemaphoreType.DMA
     bf16, f32 = jnp.bfloat16, jnp.float32
     out = pl.pallas_call(
         functools.partial(attend_kernel, (X, C, Z, Y, R, KVL, G, D)),
         out_shape=jax.ShapeDtypeStruct((C, KVL, G, X * R, D), bf16),
-        in_specs=[pl.BlockSpec(memory_space=pltpu.SMEM)] + [vmem] * 4,
-        out_specs=vmem,
+        in_specs=[hbm] * 5,
+        out_specs=hbm,
         scratch_shapes=[
+            pltpu.SMEM(run_index.shape, run_index.dtype),
+            pltpu.VMEM(freqs.shape, f32),
+            pltpu.VMEM(queries.shape, bf16),
+            pltpu.VMEM(keys.shape, bf16),
+            pltpu.VMEM(values.shape, bf16),
+            dma((5,)),
             pltpu.VMEM((X * C, 2, KVL, R, D), bf16),
             pltpu.VMEM((X * C, KVL, G, R, D), bf16),
             pltpu.VMEM((Z, Y, X, 2, KVL, C, R, D), bf16),
@@ -381,7 +415,7 @@
             dma((X, C)),
             dma((X, C)),
             dma((X, C)),
-            dma((Z, X)),
+            dma((2, Z, X)),
             dma((Z, X)),
             dma((Z, Y, X)),
             dma((Z, Y, X)),
@@ -389,7 +423,7 @@
             dma((C, X)),
         ],
         compiler_params=pltpu.CompilerParams(
-            collective_id=0, has_side_effects=True, vmem_limit_bytes=48 * 2**20
+            collective_id=0, has_side_effects=True, vmem_limit_bytes=64 * 2**20
         ),
     )(run_index, freqs, queries, keys, values)
     return jnp.transpose(out.reshape(C * KVL * G, X * R, D), (1, 0, 2))

time: 33 us -> 30.2 us (0.915)
  local copies, waits for them, and re-layouts: 4.81 us -> 1.83 us
    unnamed x10 -> x0, local copies, waits for them, and re-layouts: 3.94 us -> none
    reshape x1, local copies, waits for them, and re-layouts: 0.88 us -> 1.83 us  [per_device(): return jnp.transpose(out.reshape(C * KVL * G, X * R, D), (1, 0, 2))]
where the time goes in v2:
time: 30.2 us; the launch traced here: 30 us
  Pallas kernels  28.2 us (93%)
  local copies, waits for them, and re-layouts  1.83 us (6%)
    pallas_call x1, Pallas kernels, per_device(): pl.pallas_call(functools.partial(attend_kernel, (X, C, Z, Y, R, KVL, G, D...  28.2 us
    reshape x1, local copies, waits for them, and re-layouts, per_device(): return jnp.transpose(out.reshape(C * KVL * G, X * R, D), (1, 0, 2))  1.83 us

profile of v2, /device:TPU:0, one launch (start us, length us, event | category | flops | bytes accessed | tf_op | source)
XLA Modules:
  0.0 30.0 jit_solution(15336341908943586394)
XLA Ops:
  0.0 28.2 %shard_map.55 = bf16[2,2,4,64,128]{4,3,2,1,0:T(8,128)(2,1)} custom-call(s32[16]{0:T(128)} %run_hbm.1, f32[1,128]{1,0:T(1,128)} %constant.2.clone.freq_hbm, bf16[1,32,32,128]{3,2,1,0:T(8,128)(2,1)} %q_hbm.1, bf16[1,32,8,128]{3,2,1,0:T(8,128)(2,1)} %k_hbm.1, bf16[1,32,8,128]{3,2,1,0:T(8,128)(2,1)} %v_hbm.1), custom_call_target="tpu_custom_call" | custom-call | tf_op jit(solution)/shard_map/pallas_call | solution.py:394
  28.2 1.8 %copy.8 = bf16[16,64,128]{2,0,1:T(8,128)(2,1)} copy(bf16[16,64,128]{2,1,0:T(8,128)(2,1)} %bitcast.4) | data formatting | bytes 524288 | tf_op jit(solution)/shard_map/reshape | solution.py:429

commit v3 on v2

--- a/solution.py
+++ b/solution.py
@@ -56,6 +56,7 @@
     acc_ref,
     max_ref,
     sum_ref,
+    pos_ref,
     out_part,
     kv_send,
     kv_recv,
@@ -150,7 +151,7 @@
         rotated(by_head(k_ref, 0, kv_heads)).astype(jnp.bfloat16).reshape(X * C, KVL, R, D)
     )
     kv_out[:, 1] = by_head(v_ref, 0, kv_heads).astype(jnp.bfloat16).reshape(X * C, KVL, R, D)
-    kv_all[z, 0, x, :, :, c] = kv_out[mine]
+    kv_all[z, 0, x, c] = kv_out[mine]
 
     pl.semaphore_wait(barrier, len(offsets) + Y - 1 + jnp.minimum(z, 1) + jnp.minimum(Z - 1 - z, 1))
 
@@ -164,11 +165,38 @@
             device_id_type=pl.DeviceIdType.MESH,
         )
 
+    units_here = [
+        ((x + X - dx) % X, (c + C - dc) % C) for dx in range(X) for dc in range(C)
+    ]
+
+    def z_copy(at, up, unit):
+        return remote(
+            kv_all.at[at, 0, *unit],
+            kv_all.at[at, 0, *unit],
+            z_send.at[up, at, *unit],
+            z_recv.at[at, *unit],
+            device(x, c, b + Y if up else b - Y),
+        )
+
+    def y_copy(at, m, unit):
+        return remote(
+            kv_all.at[at, 0, *unit],
+            kv_all.at[at, m, *unit],
+            y_send.at[at, m, *unit],
+            y_recv.at[at, m, *unit],
+            device(x, c, z * Y + y_to(m)),
+        )
+
+    def pass_on(at, unit):
+        pl.when((at <= z) & (z < Z - 1))(lambda: z_copy(at, 1, unit).start())
+        pl.when((at >= z) & (z > 0))(lambda: z_copy(at, 0, unit).start())
+        small_loop(1, Y, lambda m: y_copy(at, m, unit).start())
+
     def kv_copy(dx, dc):
         xx, cc = (x + dx) % X, (c + dc) % C
         return remote(
             kv_out.at[xx * C + cc],
-            kv_all.at[z, 0, x, :, :, c],
+            kv_all.at[z, 0, x, c],
             kv_send.at[dx, dc],
             kv_recv.at[dx, dc],
             device(xx, cc, b),
@@ -186,6 +214,7 @@
 
     for dx, dc in offsets:
         kv_copy(dx, dc).start()
+    pass_on(z, units_here[0])
 
     loads[4].wait()
     q_heads = KVL * G
@@ -198,44 +227,15 @@
     q_all[x, :, c] = q_out[mine]
     for dx, dc in offsets:
         q_copy(dx, dc).start()
-
-    def z_copy(at, up, piece):
-        return remote(
-            kv_all.at[at, 0, piece],
-            kv_all.at[at, 0, piece],
-            z_send.at[up, at, piece],
-            z_recv.at[at, piece],
-            device(x, c, b + Y if up else b - Y),
-        )
-
-    def y_copy(at, m, piece):
-        return remote(
-            kv_all.at[at, 0, piece],
-            kv_all.at[at, m, piece],
-            y_send.at[at, m, piece],
-            y_recv.at[at, m, piece],
-            device(x, c, z * Y + y_to(m)),
-        )
-
-    def piece_at(dx):
-        return (x + X - dx) % X
-
-    def pass_on(at, piece):
-        pl.when((at <= z) & (z < Z - 1))(lambda: z_copy(at, 1, piece).start())
-        pl.when((at >= z) & (z > 0))(lambda: z_copy(at, 0, piece).start())
-        small_loop(1, Y, lambda m: y_copy(at, m, piece).start())
-
-    for dx in range(X):
-        for dc in range(C):
-            if (dx, dc) != (0, 0):
-                kv_copy(dx, dc).wait_recv()
-        pass_on(z, piece_at(dx))
+    for (dx, dc), unit in zip(offsets, units_here[1:]):
+        kv_copy(dx, dc).wait_recv()
+        pass_on(z, unit)
 
     def receive(k):
         at = z_near(k)
-        for dx in range(X):
-            z_copy(at, 1, piece_at(dx)).wait_recv()
-            pass_on(at, piece_at(dx))
+        for unit in units_here:
+            z_copy(at, 1, unit).wait_recv()
+            pass_on(at, unit)
 
     scaling = math.log2(math.e) * D ** (-0.5)
 
@@ -254,12 +254,15 @@
         return total
 
     def query_positions(piece):
-        row = lax.broadcasted_iota(jnp.int32, (rows, 1), 0)
+        row = lax.broadcasted_iota(jnp.int32, (rows, D), 0)
         total = row % R
         for t in range(C):
             total = total + jnp.where(row // (G * R) == t, first_pos(t * (Z * Y) + b, piece), 0)
         return total
 
+    for piece in range(X):
+        pos_ref[piece] = query_positions(piece)
+
     early = list(range(X // 2))
     late = list(range(X // 2, X))
 
@@ -268,7 +271,12 @@
 
         def units(kind, head, pieces):
             return jnp.concatenate(
-                [kv_all[at, m, p, kind, head].reshape(C * R, D) for p in pieces for m in range(Y)],
+                [
+                    kv_all[at, m, p, t, kind, head]
+                    for p in pieces
+                    for m in range(Y)
+                    for t in range(C)
+                ],
                 axis=0,
             )
 
@@ -278,7 +286,6 @@
             values = {"early": units(1, head, early), "late": units(1, head, late)}
             for piece in range(X):
                 query = q_all[piece, head].reshape(rows, D)
-                query_pos = query_positions(piece)
                 own = "early" if piece in early else "late"
                 parts = ["early"] if own == "early" else ["early", "late"]
                 scores = []
@@ -287,23 +294,24 @@
                         query, keys[part], (((1,), (1,)), ((), ())),
                         preferred_element_type=jnp.float32,
                     )
-                    if part == own:
-                        s = jnp.where(key_pos[part] <= query_pos, s, mask_floor)
-                    scores.append(s)
-                top = functools.reduce(
-                    jnp.maximum, [jnp.max(s, axis=-1, keepdims=True) for s in scores]
-                )
+                    for start in range(0, s.shape[1], D):
+                        column = s[:, start : start + D]
+                        if part == own:
+                            seen = key_pos[part][:, start : start + D] <= pos_ref[piece]
+                            column = jnp.where(seen, column, mask_floor)
+                        scores.append(column)
+                top = jnp.max(functools.reduce(jnp.maximum, scores), axis=-1, keepdims=True)
+                top = jnp.broadcast_to(top, (rows, D))
                 if not first:
                     before = max_ref[piece, head]
                     top = jnp.maximum(top, before)
                     factor = jnp.exp2((before - top) * scaling)
                 weights = [jnp.exp2((s - top) * scaling) for s in scores]
-                total = sum(jnp.sum(w, axis=-1, keepdims=True) for w in weights)
-                update = sum(
-                    jnp.dot(
-                        w.astype(jnp.bfloat16), values[part], preferred_element_type=jnp.float32
-                    )
-                    for w, part in zip(weights, parts)
+                total = sum(weights)
+                update = jnp.dot(
+                    jnp.concatenate([w.astype(jnp.bfloat16) for w in weights], axis=1),
+                    jnp.concatenate([values[part] for part in parts], axis=0),
+                    preferred_element_type=jnp.float32,
                 )
                 if not first:
                     total = total + sum_ref[piece, head] * factor
@@ -319,9 +327,8 @@
         q_copy(dx, dc).wait_recv()
 
     def arrive(k):
-        for dx in range(X):
-            piece = piece_at(dx)
-            small_loop(1, Y, lambda m: y_copy(z_near(k), m, piece).wait_recv())
+        for unit in units_here:
+            small_loop(1, Y, lambda m: y_copy(z_near(k), m, unit).wait_recv())
 
     arrive(0)
     attend(0, True)
@@ -347,34 +354,28 @@
             device(x, cc, b),
         )
 
-    def own_copy(piece):
-        return pltpu.make_async_copy(
-            out_part.at[piece, c], out_ref.at[c, :, :, pl.ds(piece * R, R)], o_send.at[0, piece]
-        )
-
     for piece in range(X):
         for head in range(KVL):
-            mixed = acc_ref[piece, head] / sum_ref[piece, head]
+            mixed = acc_ref[piece, head] / jnp.sum(sum_ref[piece, head], axis=-1, keepdims=True)
             out_part[piece, :, head] = mixed.astype(jnp.bfloat16).reshape(C, G, R, D)
         for dc in range(1, C):
             o_copy(dc, piece).start()
-        own_copy(piece).start()
+        out_ref[c, :, :, pl.ds(piece * R, R)] = out_part[piece, c]
 
     for dx, dc in offsets:
         kv_copy(dx, dc).wait_send()
         q_copy(dx, dc).wait_send()
-    for piece in range(X):
+    for unit in units_here:
 
         def sent(at):
-            pl.when((at <= z) & (z < Z - 1))(lambda: z_copy(at, 1, piece).wait_send())
-            pl.when((at >= z) & (z > 0))(lambda: z_copy(at, 0, piece).wait_send())
-            small_loop(1, Y, lambda m: y_copy(at, m, piece).wait_send())
+            pl.when((at <= z) & (z < Z - 1))(lambda: z_copy(at, 1, unit).wait_send())
+            pl.when((at >= z) & (z > 0))(lambda: z_copy(at, 0, unit).wait_send())
+            small_loop(1, Y, lambda m: y_copy(at, m, unit).wait_send())
 
         small_loop(0, Z, sent)
     for piece in range(X):
         for dc in range(1, C):
             o_copy(dc, piece).wait()
-        own_copy(piece).wait()
 
 
 def per_device(queries, keys, values, run_index):
@@ -393,9 +394,9 @@
     bf16, f32 = jnp.bfloat16, jnp.float32
     out = pl.pallas_call(
         functools.partial(attend_kernel, (X, C, Z, Y, R, KVL, G, D)),
-        out_shape=jax.ShapeDtypeStruct((C, KVL, G, X * R, D), bf16),
+        out_shape=pltpu.VMEM((C, KVL, G, X * R, D), bf16),
         in_specs=[hbm] * 5,
-        out_specs=hbm,
+        out_specs=pl.BlockSpec(memory_space=pltpu.VMEM),
         scratch_shapes=[
             pltpu.SMEM(run_index.shape, run_index.dtype),
             pltpu.VMEM(freqs.shape, f32),
@@ -405,25 +406,26 @@
             dma((5,)),
             pltpu.VMEM((X * C, 2, KVL, R, D), bf16),
             pltpu.VMEM((X * C, KVL, G, R, D), bf16),
-            pltpu.VMEM((Z, Y, X, 2, KVL, C, R, D), bf16),
+            pltpu.VMEM((Z, Y, X, C, 2, KVL, R, D), bf16),
             pltpu.VMEM((X, KVL, C, G, R, D), bf16),
             pltpu.VMEM((X, KVL, rows, D), f32),
-            pltpu.VMEM((X, KVL, rows, 1), f32),
-            pltpu.VMEM((X, KVL, rows, 1), f32),
+            pltpu.VMEM((X, KVL, rows, D), f32),
+            pltpu.VMEM((X, KVL, rows, D), f32),
+            pltpu.VMEM((X, rows, D), jnp.int32),
             pltpu.VMEM((X, C, KVL, G, R, D), bf16),
             dma((X, C)),
             dma((X, C)),
             dma((X, C)),
             dma((X, C)),
-            dma((2, Z, X)),
-            dma((Z, X)),
-            dma((Z, Y, X)),
-            dma((Z, Y, X)),
+            dma((2, Z, X, C)),
+            dma((Z, X, C)),
+            dma((Z, Y, X, C)),
+            dma((Z, Y, X, C)),
             dma((C, X)),
             dma((C, X)),
         ],
         compiler_params=pltpu.CompilerParams(
-            collective_id=0, has_side_effects=True, vmem_limit_bytes=64 * 2**20
+            collective_id=0, has_side_effects=True, vmem_limit_bytes=60 * 2**20
         ),
     )(run_index, freqs, queries, keys, values)
     return jnp.transpose(out.reshape(C * KVL * G, X * R, D), (1, 0, 2))

time: 30.2 us -> 27.2 us (0.901)
  Pallas kernels: 28.2 us -> 26.1 us
  local copies, waits for them, and re-layouts: 1.83 us -> 0.88 us
    pallas_call x1, Pallas kernels: 28.2 us -> 26.1 us  [per_device(): pl.pallas_call(functools.partial(attend_kernel, (X, C, Z, Y, R, KVL, G, D...]
    reshape x1, local copies, waits for them, and re-layouts: 1.83 us -> 0.88 us  [per_device(): return jnp.transpose(out.reshape(C * KVL * G, X * R, D), (1, 0, 2))]
where the time goes in v3:
time: 27.2 us; the launch traced here: 27 us
  Pallas kernels  26.1 us (96%)
  local copies, waits for them, and re-layouts  0.88 us (3%)
    pallas_call x1, Pallas kernels, per_device(): pl.pallas_call(functools.partial(attend_kernel, (X, C, Z, Y, R, KVL, G, D...  26.1 us
    reshape x1, local copies, waits for them, and re-layouts, per_device(): return jnp.transpose(out.reshape(C * KVL * G, X * R, D), (1, 0, 2))  0.88 us

profile of v3, /device:TPU:0, one launch (start us, length us, event | category | flops | bytes accessed | tf_op | source)
XLA Modules:
  0.0 27.0 jit_solution(9828733012167417702)
XLA Ops:
  0.0 26.1 %shard_map.55 = bf16[2,2,4,64,128]{4,3,2,1,0:T(8,128)(2,1)S(1)} custom-call(s32[16]{0:T(128)} %run_hbm.1, f32[1,128]{1,0:T(1,128)} %constant.2.clone.freq_hbm, bf16[1,32,32,128]{3,2,1,0:T(8,128)(2,1)} %q_hbm.1, bf16[1,32,8,128]{3,2,1,0:T(8,128)(2,1)} %k_hbm.1, bf16[1,32,8,128]{3,2,1,0:T(8,128)(2,1)} %v_hbm.1), custom_call_target="tpu_custom_call" | custom-call | tf_op jit(solution)/shard_map/pallas_call | solution.py:395
  26.1 0.9 %copy.8 = bf16[16,64,128]{2,0,1:T(8,128)(2,1)} copy(bf16[16,64,128]{2,1,0:T(8,128)(2,1)S(1)} %bitcast.4) | data formatting | bytes 524288 | tf_op jit(solution)/shard_map/reshape | solution.py:431

commit v4 on v3

v4 whole, which is shorter than its diff:
```python
import functools
import math

import jax
import jax.numpy as jnp
import numpy as np
from jax import lax
from jax.experimental import pallas as pl
from jax.experimental.pallas import tpu as pltpu
from jax.sharding import PartitionSpec as P

mask_floor = -1e30
rope_theta = 500000.0
rope_factor = 8.0
low_factor = 1.0
high_factor = 4.0
initial_context = 8192.0


def inverse_freqs(head_width):
    counter = np.arange(head_width // 2, dtype=np.float64)
    base_freq = 1.0 / rope_theta ** (2.0 * counter / head_width)
    wavelength = 2.0 * np.pi / base_freq
    smooth = (initial_context / wavelength - low_factor) / (high_factor - low_factor)
    blended = (1.0 - smooth) * base_freq / rope_factor + smooth * base_freq
    middle = np.where(wavelength > initial_context / low_factor, base_freq / rope_factor, blended)
    return np.where(wavelength < initial_context / high_factor, base_freq, middle)


def small_loop(first, last, body):
    if last - first <= 4:
        for at in range(first, last):
            body(at)
    else:
        lax.fori_loop(first, last, lambda at, unused: (body(at), unused)[1], 0)


def attend_kernel(
    dims,
    run_hbm,
    freq_hbm,
    q_hbm,
    k_hbm,
    v_hbm,
    out_ref,
    run_ref,
    freq_ref,
    q_ref,
    k_ref,
    v_ref,
    load_sem,
    kv_out,
    q_out,
    kv_all,
    q_all,
    acc_ref,
    max_ref,
    sum_ref,
    pos_ref,
    out_part,
    kv_send,
    kv_recv,
    q_send,
    q_recv,
    z_send,
    z_recv,
    o_send,
    o_recv,
):
    X, C, Z, Y, R, KVL, G, D = dims
    S = C * Z * Y
    half = X * R // 2
    rows = C * G * R
    x, c, b = lax.axis_index("heads"), lax.axis_index("team"), lax.axis_index("blk")
    z, y = b // Y, b % Y
    mine = (x * Y + y) * C + c
    def device(xx, cc, bb):
        return {"heads": xx, "team": cc, "blk": bb}

    loads = [
        pltpu.make_async_copy(src, dst, load_sem.at[at])
        for at, (src, dst) in enumerate(
            [(run_hbm, run_ref), (freq_hbm, freq_ref), (k_hbm, k_ref), (v_hbm, v_ref), (q_hbm, q_ref)]
        )
    ]
    for load in loads:
        load.start()

    low, high = z, Z - 1 - z
    near = jnp.minimum(low, high)

    def z_near(k):
        if isinstance(k, int) and k == 0:
            return z
        paired = jnp.where(k % 2 == 1, z - (k + 1) // 2, z + k // 2)
        single = jnp.where(low < high, z + (k - near), z - (k - near))
        return jnp.where(k <= 2 * near, paired, single)

    offsets = [
        (dx, dy, dc)
        for dx in range(X)
        for dy in range(Y)
        for dc in range(C)
        if (dx, dy, dc) != (0, 0, 0)
    ]

    barrier = pltpu.get_barrier_semaphore()

    def greet(xx, cc, bb):
        pl.semaphore_signal(
            barrier, inc=1, device_id=device(xx, cc, bb), device_id_type=pl.DeviceIdType.MESH
        )

    def member(dx, dy, dc):
        return (x + dx) % X, (y + dy) % Y, (c + dc) % C

    for offset in offsets:
        xx, yy, cc = member(*offset)
        greet(xx, cc, z * Y + yy)
    pl.when(z > 0)(lambda: greet(x, c, b - Y))
    pl.when(z < Z - 1)(lambda: greet(x, c, b + Y))

    def first_pos(slot, piece):
        run = run_ref[slot]
        start = piece * R
        if isinstance(piece, int):
            return run * half + start if start < half else (2 * S - 1 - run) * half + start - half
        return jnp.where(start < half, run * half, (2 * S - 1 - run) * half - half) + start

    loads[0].wait()
    loads[1].wait()

    own_first = first_pos(c * (Z * Y) + b, x)
    pos = own_first + lax.broadcasted_iota(jnp.int32, (R, D), 0)
    angles = pos.astype(jnp.float32) * freq_ref[...]
    cosine = jnp.cos(angles)
    sine = jnp.sin(angles)
    lanes = lax.broadcasted_iota(jnp.int32, (R, D), 1)
    sine = jnp.where(lanes < D // 2, -sine, sine)

    def by_head(ref, first, count):
        return jnp.swapaxes(ref[0, :, first : first + count, :].astype(jnp.float32), 0, 1)

    def rotated(values):
        turned = pltpu.roll(values, D // 2, 2)
        return values * cosine[None] + turned * sine[None]

    loads[2].wait()
    loads[3].wait()
    kv_heads = X * Y * C * KVL
    kv_out[:, 0] = (
        rotated(by_head(k_ref, 0, kv_heads)).astype(jnp.bfloat16).reshape(X * Y * C, KVL, R, D)
    )
    kv_out[:, 1] = by_head(v_ref, 0, kv_heads).astype(jnp.bfloat16).reshape(X * Y * C, KVL, R, D)
    kv_all[z, x, y, c] = kv_out[mine]

    pl.semaphore_wait(barrier, len(offsets) + jnp.minimum(z, 1) + jnp.minimum(Z - 1 - z, 1))

    def remote(src, dst, send, recv, to):
        return pltpu.make_async_remote_copy(
            src_ref=src,
            dst_ref=dst,
            send_sem=send,
            recv_sem=recv,
            device_id=to,
            device_id_type=pl.DeviceIdType.MESH,
        )

    units_here = [((x + X - dx) % X, (y + Y - dy) % Y) for dx in range(X) for dy in range(Y)]

    def z_copy(at, up, unit):
        return remote(
            kv_all.at[at, *unit],
            kv_all.at[at, *unit],
            z_send.at[up, at, *unit],
            z_recv.at[at, *unit],
            device(x, c, b + Y if up else b - Y),
        )

    def pass_on(at, unit):
        pl.when((at <= z) & (z < Z - 1))(lambda: z_copy(at, 1, unit).start())
        pl.when((at >= z) & (z > 0))(lambda: z_copy(at, 0, unit).start())

    def kv_copy(*offset):
        xx, yy, cc = member(*offset)
        return remote(
            kv_out.at[(xx * Y + yy) * C + cc],
            kv_all.at[z, x, y, c],
            kv_send.at[*offset],
            kv_recv.at[*offset],
            device(xx, cc, z * Y + yy),
        )

    def q_copy(*offset):
        xx, yy, cc = member(*offset)
        return remote(
            q_out.at[(xx * Y + yy) * C + cc],
            q_all.at[x, :, y, c],
            q_send.at[*offset],
            q_recv.at[*offset],
            device(xx, cc, z * Y + yy),
        )

    for offset in offsets:
        kv_copy(*offset).start()

    loads[4].wait()
    q_heads = KVL * G
    for to in range(X * Y * C):
        q_out[to] = (
            rotated(by_head(q_ref, to * q_heads, q_heads))
            .astype(jnp.bfloat16)
            .reshape(KVL, G, R, D)
        )
    q_all[x, :, y, c] = q_out[mine]
    for offset in offsets:
        q_copy(*offset).start()
    for dx in range(X):
        for dy in range(Y):
            for dc in range(C):
                if (dx, dy, dc) != (0, 0, 0):
                    kv_copy(dx, dy, dc).wait_recv()
            pass_on(z, units_here[dx * Y + dy])

    def receive(k):
        at = z_near(k)
        for unit in units_here:
            z_copy(at, 1, unit).wait_recv()
            pass_on(at, unit)

    scaling = math.log2(math.e) * D ** (-0.5)

    def key_positions(k, pieces):
        count = len(pieces) * Y * C * R
        lane = lax.broadcasted_iota(jnp.int32, (1, count), 1)
        segment = lane // R
        total = lane % R
        at = 0
        for piece in pieces:
            for yy in range(Y):
                for cc in range(C):
                    slot = cc * (Z * Y) + z_near(k) * Y + yy
                    total = total + jnp.where(segment == at, first_pos(slot, piece), 0)
                    at += 1
        return total

    def query_positions(piece, yy):
        row = lax.broadcasted_iota(jnp.int32, (rows, D), 0)
        total = row % R
        for cc in range(C):
            slot = cc * (Z * Y) + z * Y + yy
            total = total + jnp.where(row // (G * R) == cc, first_pos(slot, piece), 0)
        return total

    for piece in range(X):
        for yy in range(Y):
            pos_ref[piece, yy] = query_positions(piece, yy)

    early = list(range(X // 2))
    late = list(range(X // 2, X))

    def attend(k, first, last):
        at = z_near(k)

        def units(kind, head, pieces):
            return jnp.concatenate(
                [
                    kv_all[at, p, yy, cc, kind, head]
                    for p in pieces
                    for yy in range(Y)
                    for cc in range(C)
                ],
                axis=0,
            )

        key_pos = {"early": key_positions(k, early), "late": key_positions(k, late)}
        for piece in range(X):
            own = "early" if piece in early else "late"
            parts = ["early"] if own == "early" else ["early", "late"]
            for dy in reversed(range(Y)):
                yy = (y + dy) % Y
                for head in range(KVL):
                    query = q_all[piece, head, yy].reshape(rows, D)
                    scores = []
                    for part in parts:
                        s = lax.dot_general(
                            query,
                            units(0, head, early if part == "early" else late),
                            (((1,), (1,)), ((), ())),
                            preferred_element_type=jnp.float32,
                        )
                        width = math.gcd(s.shape[1], D)
                        for start in range(0, s.shape[1], width):
                            column = s[:, start : start + width]
                            if part == own:
                                seen_to = pos_ref[piece, yy, :, :width]
                                seen = key_pos[part][:, start : start + width] <= seen_to
                                column = jnp.where(seen, column, mask_floor)
                            scores.append(column)
                    top = jnp.max(functools.reduce(jnp.maximum, scores), axis=-1, keepdims=True)
                    top = jnp.broadcast_to(top, (rows, D))
                    if not first:
                        before = max_ref[piece, head, yy]
                        top = jnp.maximum(top, before)
                        factor = jnp.exp2((before - top) * scaling)
                    weights = [jnp.exp2((s - top[:, :width]) * scaling) for s in scores]
                    total = sum(weights)
                    shared = units(1, head, early if own == "early" else early + late)
                    if width == D:
                        weights = [jnp.concatenate([w.astype(jnp.bfloat16) for w in weights], axis=1)]
                    else:
                        total = jnp.concatenate([total, jnp.zeros((rows, D - width), total.dtype)], axis=1)
                    update, start = 0.0, 0
                    for w in weights:
                        update = update + jnp.dot(
                            w.astype(jnp.bfloat16),
                            shared[start : start + w.shape[1]],
                            preferred_element_type=jnp.float32,
                        )
                        start += w.shape[1]
                    if not first:
                        total = total + sum_ref[piece, head, yy] * factor
                        update = update + acc_ref[piece, head, yy] * factor
                    if last:
                        mixed = update / jnp.sum(total, axis=-1, keepdims=True)
                        out_part[piece, yy, :, head] = mixed.astype(jnp.bfloat16).reshape(
                            C, G, R, D
                        )
                    else:
                        max_ref[piece, head, yy] = top
                        sum_ref[piece, head, yy] = total
                        acc_ref[piece, head, yy] = update
                if last:
                    for dc in reversed(range(C)):
                        if (dy, dc) != (0, 0):
                            o_copy(dy, dc, piece).start()
                        else:
                            out_ref[y * C + c, :, :, pl.ds(piece * R, R)] = out_part[piece, y, c]

    def o_copy(dy, dc, piece):
        xx, yy, cc = member(0, dy, dc)
        return remote(
            out_part.at[piece, yy, cc],
            out_ref.at[y * C + c, :, :, pl.ds(piece * R, R)],
            o_send.at[dy, dc, piece],
            o_recv.at[dy, dc, piece],
            device(x, cc, z * Y + yy),
        )

    if Z > 1:
        receive(1)
    for offset in offsets:
        q_copy(*offset).wait_recv()
    attend(0, True, Z == 1)

    def later(k):
        receive(k + 1)
        attend(k, False, False)

    small_loop(1, Z - 1, later)
    if Z > 1:
        attend(Z - 1, False, True)

    for offset in offsets:
        kv_copy(*offset).wait_send()
        q_copy(*offset).wait_send()
    for unit in units_here:

        def sent(at):
            pl.when((at <= z) & (z < Z - 1))(lambda: z_copy(at, 1, unit).wait_send())
            pl.when((at >= z) & (z > 0))(lambda: z_copy(at, 0, unit).wait_send())

        small_loop(0, Z, sent)
    for dx, dy, dc in offsets:
        if dx == 0:
            for piece in range(X):
                o_copy(dy, dc, piece).wait()


def per_device(queries, keys, values, run_index):
    X, C, B = lax.axis_size("heads"), lax.axis_size("team"), lax.axis_size("blk")
    R, QH, D = queries.shape[1:]
    KVH = keys.shape[2]
    Y = math.gcd(KVH // (X * C), B)
    KVL = KVH // (X * C * Y)
    G = QH // KVH
    Z = B // Y
    freqs = inverse_freqs(D)
    freqs = jnp.asarray(np.concatenate([freqs, freqs])[None], jnp.float32)
    rows = C * G * R
    hbm = pl.BlockSpec(memory_space=pltpu.HBM)
    dma = pltpu.SemaphoreType.DMA
    bf16, f32 = jnp.bfloat16, jnp.float32
    out = pl.pallas_call(
        functools.partial(attend_kernel, (X, C, Z, Y, R, KVL, G, D)),
        out_shape=pltpu.VMEM((Y * C, KVL, G, X * R, D), bf16),
        in_specs=[hbm] * 5,
        out_specs=pl.BlockSpec(memory_space=pltpu.VMEM),
        scratch_shapes=[
            pltpu.SMEM(run_index.shape, run_index.dtype),
            pltpu.VMEM(freqs.shape, f32),
            pltpu.VMEM(queries.shape, bf16),
            pltpu.VMEM(keys.shape, bf16),
            pltpu.VMEM(values.shape, bf16),
            dma((5,)),
            pltpu.VMEM((X * Y * C, 2, KVL, R, D), bf16),
            pltpu.VMEM((X * Y * C, KVL, G, R, D), bf16),
            pltpu.VMEM((Z, X, Y, C, 2, KVL, R, D), bf16),
            pltpu.VMEM((X, KVL, Y, C, G, R, D), bf16),
            pltpu.VMEM((X, KVL, Y, rows, D), f32),
            pltpu.VMEM((X, KVL, Y, rows, D), f32),
            pltpu.VMEM((X, KVL, Y, rows, D), f32),
            pltpu.VMEM((X, Y, rows, D), jnp.int32),
            pltpu.VMEM((X, Y, C, KVL, G, R, D), bf16),
            dma((X, Y, C)),
            dma((X, Y, C)),
            dma((X, Y, C)),
            dma((X, Y, C)),
            dma((2, Z, X, Y)),
            dma((Z, X, Y)),
            dma((Y, C, X)),
            dma((Y, C, X)),
        ],
        compiler_params=pltpu.CompilerParams(
            collective_id=0, has_side_effects=True, vmem_limit_bytes=60 * 2**20
        ),
    )(run_index, freqs, queries, keys, values)
    return jnp.transpose(out.reshape(Y * C * KVL * G, X * R, D), (1, 0, 2))


def solution(mesh):
    in_specs = (
        P("heads", ("team", "blk"), None, None),
        P("heads", ("team", "blk"), None, None),
        P("heads", ("team", "blk"), None, None),
        P(),
    )
    out_specs = P(("team", "blk"), "heads", None)
    return jax.shard_map(
        per_device, mesh=mesh, in_specs=in_specs, out_specs=out_specs, check_vma=False
    )
```

time: 27.2 us -> 27.7 us (1.018)
  Pallas kernels: 26.1 us -> 26.6 us
    pallas_call x1, Pallas kernels: 26.1 us -> 26.6 us  [per_device(): pl.pallas_call(functools.partial(attend_kernel, (X, C, Z, Y, R, KVL, G, D...]
where the time goes in v4:
time: 27.7 us; the launch traced here: 27.5 us
  Pallas kernels  26.6 us (96%)
  local copies, waits for them, and re-layouts  0.88 us (3%)
    pallas_call x1, Pallas kernels, per_device(): pl.pallas_call(functools.partial(attend_kernel, (X, C, Z, Y, R, KVL, G, D...  26.6 us
    reshape x1, local copies, waits for them, and re-layouts, per_device(): return jnp.transpose(out.reshape(Y * C * KVL * G, X * R, D), (1, 0, 2))  0.88 us

profile of v4, /device:TPU:0, one launch (start us, length us, event | category | flops | bytes accessed | tf_op | source)
XLA Modules:
  0.0 27.5 jit_solution(13481943075115381603)
XLA Ops:
  0.0 26.6 %shard_map.55 = bf16[4,1,4,64,128]{4,3,2,1,0:T(8,128)(2,1)S(1)} custom-call(s32[16]{0:T(128)} %run_hbm.1, f32[1,128]{1,0:T(1,128)} %constant.2.clone.freq_hbm, bf16[1,32,32,128]{3,2,1,0:T(8,128)(2,1)} %q_hbm.1, bf16[1,32,8,128]{3,2,1,0:T(8,128)(2,1)} %k_hbm.1, bf16[1,32,8,128]{3,2,1,0:T(8,128)(2,1)} %v_hbm.1), custom_call_target="tpu_custom_call" | custom-call | tf_op jit(solution)/shard_map/pallas_call | solution.py:394
  26.6 0.9 %copy.8 = bf16[16,64,128]{2,0,1:T(8,128)(2,1)} copy(bf16[16,64,128]{2,1,0:T(8,128)(2,1)S(1)} %bitcast.4) | data formatting | bytes 524288 | tf_op jit(solution)/shard_map/reshape | solution.py:428

commit v5 on v4

--- a/solution.py
+++ b/solution.py
@@ -86,15 +86,14 @@
     for load in loads:
         load.start()
 
-    low, high = z, Z - 1 - z
-    near = jnp.minimum(low, high)
-
-    def z_near(k):
-        if isinstance(k, int) and k == 0:
-            return z
-        paired = jnp.where(k % 2 == 1, z - (k + 1) // 2, z + k // 2)
-        single = jnp.where(low < high, z + (k - near), z - (k - near))
-        return jnp.where(k <= 2 * near, paired, single)
+    whole_way = (Z - 1) // 2
+    up, down = (z + 1) % Z, (z + Z - 1) % Z
+
+    def below(d):
+        return (z + Z - d) % Z
+
+    def above(d):
+        return (z + d) % Z
 
     offsets = [
         (dx, dy, dc)
@@ -117,8 +116,9 @@
     for offset in offsets:
         xx, yy, cc = member(*offset)
         greet(xx, cc, z * Y + yy)
-    pl.when(z > 0)(lambda: greet(x, c, b - Y))
-    pl.when(z < Z - 1)(lambda: greet(x, c, b + Y))
+    if Z > 1:
+        greet(x, c, up * Y + y)
+        greet(x, c, down * Y + y)
 
     def first_pos(slot, piece):
         run = run_ref[slot]
@@ -154,7 +154,7 @@
     kv_out[:, 1] = by_head(v_ref, 0, kv_heads).astype(jnp.bfloat16).reshape(X * Y * C, KVL, R, D)
     kv_all[z, x, y, c] = kv_out[mine]
 
-    pl.semaphore_wait(barrier, len(offsets) + jnp.minimum(z, 1) + jnp.minimum(Z - 1 - z, 1))
+    pl.semaphore_wait(barrier, len(offsets) + (2 if Z > 1 else 0))
 
     def remote(src, dst, send, recv, to):
         return pltpu.make_async_remote_copy(
@@ -168,18 +168,25 @@
 
     units_here = [((x + X - dx) % X, (y + Y - dy) % Y) for dx in range(X) for dy in range(Y)]
 
-    def z_copy(at, up, unit):
+    def z_copy(at, upward, unit):
         return remote(
             kv_all.at[at, *unit],
             kv_all.at[at, *unit],
-            z_send.at[up, at, *unit],
+            z_send.at[upward, at, *unit],
             z_recv.at[at, *unit],
-            device(x, c, b + Y if up else b - Y),
-        )
-
-    def pass_on(at, unit):
-        pl.when((at <= z) & (z < Z - 1))(lambda: z_copy(at, 1, unit).start())
-        pl.when((at >= z) & (z > 0))(lambda: z_copy(at, 0, unit).start())
+            device(x, c, (up if upward else down) * Y + y),
+        )
+
+    def goes(d, upward, j):
+        return d <= whole_way or (2 * d == Z and j % 2 == 1 - upward)
+
+    def pass_on(at, d, upward, j):
+        if isinstance(d, int):
+            if goes(d, upward, j):
+                z_copy(at, upward, units_here[j]).start()
+        else:
+            here = (d <= whole_way) | ((2 * d == Z) & (j % 2 == 1 - upward))
+            pl.when(here)(lambda: z_copy(at, upward, units_here[j]).start())
 
     def kv_copy(*offset):
         xx, yy, cc = member(*offset)
@@ -220,28 +227,31 @@
             for dc in range(C):
                 if (dx, dy, dc) != (0, 0, 0):
                     kv_copy(dx, dy, dc).wait_recv()
-            pass_on(z, units_here[dx * Y + dy])
-
-    def receive(k):
-        at = z_near(k)
-        for unit in units_here:
-            z_copy(at, 1, unit).wait_recv()
-            pass_on(at, unit)
+            pass_on(z, 1, 1, dx * Y + dy)
+            pass_on(z, 1, 0, dx * Y + dy)
+
+    def receive(d):
+        for j, unit in enumerate(units_here):
+            z_copy(below(d), 1, unit).wait_recv()
+            pass_on(below(d), d + 1, 1, j)
+            z_copy(above(d), 0, unit).wait_recv()
+            pass_on(above(d), d + 1, 0, j)
 
     scaling = math.log2(math.e) * D ** (-0.5)
 
-    def key_positions(k, pieces):
-        count = len(pieces) * Y * C * R
+    def key_positions(planes, pieces):
+        count = len(pieces) * len(planes) * Y * C * R
         lane = lax.broadcasted_iota(jnp.int32, (1, count), 1)
         segment = lane // R
         total = lane % R
         at = 0
         for piece in pieces:
-            for yy in range(Y):
-                for cc in range(C):
-                    slot = cc * (Z * Y) + z_near(k) * Y + yy
-                    total = total + jnp.where(segment == at, first_pos(slot, piece), 0)
-                    at += 1
+            for plane in planes:
+                for yy in range(Y):
+                    for cc in range(C):
+                        slot = cc * (Z * Y) + plane * Y + yy
+                        total = total + jnp.where(segment == at, first_pos(slot, piece), 0)
+                        at += 1
         return total
 
     def query_positions(piece, yy):
@@ -259,68 +269,72 @@
     early = list(range(X // 2))
     late = list(range(X // 2, X))
 
-    def attend(k, first, last):
-        at = z_near(k)
+    def attend(planes, first, last):
 
         def units(kind, head, pieces):
             return jnp.concatenate(
                 [
-                    kv_all[at, p, yy, cc, kind, head]
+                    kv_all[plane, p, yy, cc, kind, head]
                     for p in pieces
+                    for plane in planes
                     for yy in range(Y)
                     for cc in range(C)
                 ],
                 axis=0,
             )
 
-        key_pos = {"early": key_positions(k, early), "late": key_positions(k, late)}
-        for piece in range(X):
-            own = "early" if piece in early else "late"
-            parts = ["early"] if own == "early" else ["early", "late"]
-            for dy in reversed(range(Y)):
-                yy = (y + dy) % Y
+        if planes:
+            key_pos = {"early": key_positions(planes, early), "late": key_positions(planes, late)}
+        for dy in reversed(range(Y)):
+            yy = (y + dy) % Y
+            for piece in range(X):
+                own = "early" if piece in early else "late"
+                parts = ["early"] if own == "early" else ["early", "late"]
                 for head in range(KVL):
-                    query = q_all[piece, head, yy].reshape(rows, D)
-                    scores = []
-                    for part in parts:
-                        s = lax.dot_general(
-                            query,
-                            units(0, head, early if part == "early" else late),
-                            (((1,), (1,)), ((), ())),
-                            preferred_element_type=jnp.float32,
-                        )
-                        width = math.gcd(s.shape[1], D)
-                        for start in range(0, s.shape[1], width):
-                            column = s[:, start : start + width]
-                            if part == own:
-                                seen_to = pos_ref[piece, yy, :, :width]
-                                seen = key_pos[part][:, start : start + width] <= seen_to
-                                column = jnp.where(seen, column, mask_floor)
-                            scores.append(column)
-                    top = jnp.max(functools.reduce(jnp.maximum, scores), axis=-1, keepdims=True)
-                    top = jnp.broadcast_to(top, (rows, D))
-                    if not first:
-                        before = max_ref[piece, head, yy]
-                        top = jnp.maximum(top, before)
-                        factor = jnp.exp2((before - top) * scaling)
-                    weights = [jnp.exp2((s - top[:, :width]) * scaling) for s in scores]
-                    total = sum(weights)
-                    shared = units(1, head, early if own == "early" else early + late)
-                    if width == D:
-                        weights = [jnp.concatenate([w.astype(jnp.bfloat16) for w in weights], axis=1)]
+                    if planes:
+                        query = q_all[piece, head, yy].reshape(rows, D)
+                        scores = []
+                        for part in parts:
+                            s = lax.dot_general(
+                                query,
+                                units(0, head, early if part == "early" else late),
+                                (((1,), (1,)), ((), ())),
+                                preferred_element_type=jnp.float32,
+                            )
+                            width = math.gcd(s.shape[1], D)
+                            for start in range(0, s.shape[1], width):
+                                column = s[:, start : start + width]
+                                if part == own:
+                                    seen_to = pos_ref[piece, yy, :, :width]
+                                    seen = key_pos[part][:, start : start + width] <= seen_to
+                                    column = jnp.where(seen, column, mask_floor)
+                                scores.append(column)
+                        top = jnp.max(functools.reduce(jnp.maximum, scores), axis=-1, keepdims=True)
+                        top = jnp.broadcast_to(top, (rows, D))
+                        if not first:
+                            before = max_ref[piece, head, yy]
+                            top = jnp.maximum(top, before)
+                            factor = jnp.exp2((before - top) * scaling)
+                        weights = [jnp.exp2((s - top[:, :width]) * scaling) for s in scores]
+                        total = sum(weights)
+                        shared = units(1, head, early if own == "early" else early + late)
+                        if width == D:
+                            weights = [jnp.concatenate([w.astype(jnp.bfloat16) for w in weights], axis=1)]
+                        else:
+                            total = jnp.concatenate([total, jnp.zeros((rows, D - width), total.dtype)], axis=1)
+                        update, start = 0.0, 0
+                        for w in weights:
+                            update = update + jnp.dot(
+                                w.astype(jnp.bfloat16),
+                                shared[start : start + w.shape[1]],
+                                preferred_element_type=jnp.float32,
+                            )
+                            start += w.shape[1]
+                        if not first:
+                            total = total + sum_ref[piece, head, yy] * factor
+                            update = update + acc_ref[piece, head, yy] * factor
                     else:
-                        total = jnp.concatenate([total, jnp.zeros((rows, D - width), total.dtype)], axis=1)
-                    update, start = 0.0, 0
-                    for w in weights:
-                        update = update + jnp.dot(
-                            w.astype(jnp.bfloat16),
-                            shared[start : start + w.shape[1]],
-                            preferred_element_type=jnp.float32,
-                        )
-                        start += w.shape[1]
-                    if not first:
-                        total = total + sum_ref[piece, head, yy] * factor
-                        update = update + acc_ref[piece, head, yy] * factor
+                        total, update = sum_ref[piece, head, yy], acc_ref[piece, head, yy]
                     if last:
                         mixed = update / jnp.sum(total, axis=-1, keepdims=True)
                         out_part[piece, yy, :, head] = mixed.astype(jnp.bfloat16).reshape(
@@ -347,30 +361,40 @@
             device(x, cc, z * Y + yy),
         )
 
-    if Z > 1:
+    if whole_way > 0:
         receive(1)
     for offset in offsets:
         q_copy(*offset).wait_recv()
-    attend(0, True, Z == 1)
-
-    def later(k):
-        receive(k + 1)
-        attend(k, False, False)
-
-    small_loop(1, Z - 1, later)
-    if Z > 1:
-        attend(Z - 1, False, True)
+    attend([z] + [below(1), above(1)] * min(1, whole_way), True, Z == 1)
+
+    def later(d):
+        receive(d)
+        attend([below(d), above(d)], False, False)
+
+    small_loop(2, whole_way + 1, later)
+    if Z % 2 == 0:
+        opposite = above(Z // 2)
+        for j, unit in enumerate(units_here):
+            z_copy(opposite, 1 - j % 2, unit).wait_recv()
+        attend([opposite], False, True)
+    elif Z > 1:
+        attend([], False, True)
 
     for offset in offsets:
         kv_copy(*offset).wait_send()
         q_copy(*offset).wait_send()
-    for unit in units_here:
-
-        def sent(at):
-            pl.when((at <= z) & (z < Z - 1))(lambda: z_copy(at, 1, unit).wait_send())
-            pl.when((at >= z) & (z > 0))(lambda: z_copy(at, 0, unit).wait_send())
-
-        small_loop(0, Z, sent)
+    def sent(d):
+        for j, unit in enumerate(units_here):
+            z_copy(below(d), 1, unit).wait_send()
+            z_copy(above(d), 0, unit).wait_send()
+
+    small_loop(0, whole_way, sent)
+    if Z % 2 == 0:
+        for j, unit in enumerate(units_here):
+            if j % 2 == 0:
+                z_copy(below(Z // 2 - 1), 1, unit).wait_send()
+            else:
+                z_copy(above(Z // 2 - 1), 0, unit).wait_send()
     for dx, dy, dc in offsets:
         if dx == 0:
             for piece in range(X):

time: 27.7 us -> 25.5 us (0.921)
  Pallas kernels: 26.6 us -> 24.5 us
    pallas_call x1, Pallas kernels: 26.6 us -> 24.5 us  [per_device(): pl.pallas_call(functools.partial(attend_kernel, (X, C, Z, Y, R, KVL, G, D...]
where the time goes in v5:
time: 25.5 us; the launch traced here: 25.4 us
  Pallas kernels  24.5 us (96%)
  local copies, waits for them, and re-layouts  0.88 us (3%)
    pallas_call x1, Pallas kernels, per_device(): pl.pallas_call(functools.partial(attend_kernel, (X, C, Z, Y, R, KVL, G, D...  24.5 us
    reshape x1, local copies, waits for them, and re-layouts, per_device(): return jnp.transpose(out.reshape(Y * C * KVL * G, X * R, D), (1, 0, 2))  0.88 us

profile of v5, /device:TPU:0, one launch (start us, length us, event | category | flops | bytes accessed | tf_op | source)
XLA Modules:
  0.0 25.4 jit_solution(15716906647460715912)
XLA Ops:
  0.0 24.5 %shard_map.55 = bf16[4,1,4,64,128]{4,3,2,1,0:T(8,128)(2,1)S(1)} custom-call(s32[16]{0:T(128)} %run_hbm.1, f32[1,128]{1,0:T(1,128)} %constant.2.clone.freq_hbm, bf16[1,32,32,128]{3,2,1,0:T(8,128)(2,1)} %q_hbm.1, bf16[1,32,8,128]{3,2,1,0:T(8,128)(2,1)} %k_hbm.1, bf16[1,32,8,128]{3,2,1,0:T(8,128)(2,1)} %v_hbm.1), custom_call_target="tpu_custom_call" | custom-call | tf_op jit(solution)/shard_map/pallas_call | solution.py:418
  24.5 0.9 %copy.8 = bf16[16,64,128]{2,0,1:T(8,128)(2,1)} copy(bf16[16,64,128]{2,1,0:T(8,128)(2,1)S(1)} %bitcast.4) | data formatting | bytes 524288 | tf_op jit(solution)/shard_map/reshape | solution.py:452

commit v6 on v5

--- a/solution.py
+++ b/solution.py
@@ -254,17 +254,14 @@
                         at += 1
         return total
 
-    def query_positions(piece, yy):
-        row = lax.broadcasted_iota(jnp.int32, (rows, D), 0)
-        total = row % R
-        for cc in range(C):
-            slot = cc * (Z * Y) + z * Y + yy
-            total = total + jnp.where(row // (G * R) == cc, first_pos(slot, piece), 0)
-        return total
+    def query_positions(piece, yy, cc):
+        row = lax.broadcasted_iota(jnp.int32, (R, D), 0)
+        return row + first_pos(cc * (Z * Y) + z * Y + yy, piece)
 
     for piece in range(X):
         for yy in range(Y):
-            pos_ref[piece, yy] = query_positions(piece, yy)
+            for cc in range(C):
+                pos_ref[piece, yy, cc] = query_positions(piece, yy, cc)
 
     early = list(range(X // 2))
     late = list(range(X // 2, X))
@@ -293,55 +290,71 @@
                 for head in range(KVL):
                     if planes:
                         query = q_all[piece, head, yy].reshape(rows, D)
-                        scores = []
-                        for part in parts:
-                            s = lax.dot_general(
+                        scores = [
+                            lax.dot_general(
                                 query,
                                 units(0, head, early if part == "early" else late),
                                 (((1,), (1,)), ((), ())),
                                 preferred_element_type=jnp.float32,
                             )
-                            width = math.gcd(s.shape[1], D)
-                            for start in range(0, s.shape[1], width):
-                                column = s[:, start : start + width]
-                                if part == own:
-                                    seen_to = pos_ref[piece, yy, :, :width]
-                                    seen = key_pos[part][:, start : start + width] <= seen_to
-                                    column = jnp.where(seen, column, mask_floor)
-                                scores.append(column)
-                        top = jnp.max(functools.reduce(jnp.maximum, scores), axis=-1, keepdims=True)
-                        top = jnp.broadcast_to(top, (rows, D))
-                        if not first:
-                            before = max_ref[piece, head, yy]
-                            top = jnp.maximum(top, before)
-                            factor = jnp.exp2((before - top) * scaling)
-                        weights = [jnp.exp2((s - top[:, :width]) * scaling) for s in scores]
-                        total = sum(weights)
+                            for part in parts
+                        ]
+                        width = math.gcd(scores[0].shape[1], D)
+                        rounded, totals, factors = [], [], []
+                        for at in range(0, rows, R):
+                            block = slice(at, at + R)
+                            seen_to = pos_ref[piece, yy, at // (G * R), :, :width]
+                            columns = []
+                            for part, s in zip(parts, scores):
+                                for start in range(0, s.shape[1], width):
+                                    column = s[block, start : start + width]
+                                    if part == own:
+                                        seen = key_pos[part][:, start : start + width] <= seen_to
+                                        column = jnp.where(seen, column, mask_floor)
+                                    columns.append(column)
+                            top = jnp.max(
+                                functools.reduce(jnp.maximum, columns), axis=-1, keepdims=True
+                            )
+                            top = jnp.broadcast_to(top, (R, D))
+                            if not first:
+                                before = max_ref[piece, head, yy, block]
+                                top = jnp.maximum(top, before)
+                                factors.append(jnp.exp2((before - top) * scaling))
+                            weights = [jnp.exp2((s - top[:, :width]) * scaling) for s in columns]
+                            total = sum(weights)
+                            if width < D:
+                                filler = jnp.zeros((R, D - width), total.dtype)
+                                total = jnp.concatenate([total, filler], axis=1)
+                            if not first:
+                                total = total + sum_ref[piece, head, yy, block] * factors[-1]
+                            totals.append(total)
+                            rounded.append([w.astype(jnp.bfloat16) for w in weights])
+                            if not last:
+                                max_ref[piece, head, yy, block] = top
+                        weights = [jnp.concatenate(ws, axis=0) for ws in zip(*rounded)]
+                        if width == D:
+                            weights = [jnp.concatenate(weights, axis=1)]
+                        total = jnp.concatenate(totals, axis=0)
                         shared = units(1, head, early if own == "early" else early + late)
-                        if width == D:
-                            weights = [jnp.concatenate([w.astype(jnp.bfloat16) for w in weights], axis=1)]
-                        else:
-                            total = jnp.concatenate([total, jnp.zeros((rows, D - width), total.dtype)], axis=1)
                         update, start = 0.0, 0
                         for w in weights:
                             update = update + jnp.dot(
-                                w.astype(jnp.bfloat16),
+                                w,
                                 shared[start : start + w.shape[1]],
                                 preferred_element_type=jnp.float32,
                             )
                             start += w.shape[1]
                         if not first:
-                            total = total + sum_ref[piece, head, yy] * factor
+                            factor = jnp.concatenate(factors, axis=0)
                             update = update + acc_ref[piece, head, yy] * factor
                     else:
                         total, update = sum_ref[piece, head, yy], acc_ref[piece, head, yy]
                     if last:
-                        mixed = update / jnp.sum(total, axis=-1, keepdims=True)
+                        mixed = update * (1.0 / jnp.sum(total, axis=-1, keepdims=True))
                         out_part[piece, yy, :, head] = mixed.astype(jnp.bfloat16).reshape(
                             C, G, R, D
                         )
                     else:
-                        max_ref[piece, head, yy] = top
                         sum_ref[piece, head, yy] = total
                         acc_ref[piece, head, yy] = update
                 if last:
@@ -434,7 +447,7 @@
             pltpu.VMEM((X, KVL, Y, rows, D), f32),
             pltpu.VMEM((X, KVL, Y, rows, D), f32),
             pltpu.VMEM((X, KVL, Y, rows, D), f32),
-            pltpu.VMEM((X, Y, rows, D), jnp.int32),
+            pltpu.VMEM((X, Y, C, R, D), jnp.int32),
             pltpu.VMEM((X, Y, C, KVL, G, R, D), bf16),
             dma((X, Y, C)),
             dma((X, Y, C)),

time: 25.5 us -> 25.5 us (level)
  no operation moved by 1% of the time
where the time goes in v6:
time: 25.5 us; the launch traced here: 25.4 us
  Pallas kernels  24.5 us (96%)
  local copies, waits for them, and re-layouts  0.88 us (3%)
    pallas_call x1, Pallas kernels, per_device(): pl.pallas_call(functools.partial(attend_kernel, (X, C, Z, Y, R, KVL, G, D...  24.5 us
    reshape x1, local copies, waits for them, and re-layouts, per_device(): return jnp.transpose(out.reshape(Y * C * KVL * G, X * R, D), (1, 0, 2))  0.88 us

profile of v6, /device:TPU:0, one launch (start us, length us, event | category | flops | bytes accessed | tf_op | source)
XLA Modules:
  0.0 25.4 jit_solution(1977436681757324863)
XLA Ops:
  0.0 24.5 %shard_map.55 = bf16[4,1,4,64,128]{4,3,2,1,0:T(8,128)(2,1)S(1)} custom-call(s32[16]{0:T(128)} %run_hbm.1, f32[1,128]{1,0:T(1,128)} %constant.2.clone.freq_hbm, bf16[1,32,32,128]{3,2,1,0:T(8,128)(2,1)} %q_hbm.1, bf16[1,32,8,128]{3,2,1,0:T(8,128)(2,1)} %k_hbm.1, bf16[1,32,8,128]{3,2,1,0:T(8,128)(2,1)} %v_hbm.1), custom_call_target="tpu_custom_call" | custom-call | tf_op jit(solution)/shard_map/pallas_call | solution.py:431
  24.5 0.9 %copy.8 = bf16[16,64,128]{2,0,1:T(8,128)(2,1)} copy(bf16[16,64,128]{2,1,0:T(8,128)(2,1)S(1)} %bitcast.4) | data formatting | bytes 524288 | tf_op jit(solution)/shard_map/reshape | solution.py:465

commit v7 on v6

--- a/solution.py
+++ b/solution.py
@@ -86,14 +86,16 @@
     for load in loads:
         load.start()
 
-    whole_way = (Z - 1) // 2
-    up, down = (z + 1) % Z, (z + Z - 1) % Z
-
-    def below(d):
-        return (z + Z - d) % Z
-
-    def above(d):
-        return (z + d) % Z
+    low, high = z, Z - 1 - z
+    near = jnp.minimum(low, high)
+    between = (low > 0) & (high > 0)
+
+    def z_near(k):
+        if isinstance(k, int) and k == 0:
+            return z
+        paired = jnp.where(k % 2 == 1, z - (k + 1) // 2, z + k // 2)
+        single = jnp.where(low < high, z + (k - near), z - (k - near))
+        return jnp.where(k <= 2 * near, paired, single)
 
     offsets = [
         (dx, dy, dc)
@@ -116,9 +118,8 @@
     for offset in offsets:
         xx, yy, cc = member(*offset)
         greet(xx, cc, z * Y + yy)
-    if Z > 1:
-        greet(x, c, up * Y + y)
-        greet(x, c, down * Y + y)
+    pl.when(low > 0)(lambda: greet(x, c, b - Y))
+    pl.when(high > 0)(lambda: greet(x, c, b + Y))
 
     def first_pos(slot, piece):
         run = run_ref[slot]
@@ -154,7 +155,7 @@
     kv_out[:, 1] = by_head(v_ref, 0, kv_heads).astype(jnp.bfloat16).reshape(X * Y * C, KVL, R, D)
     kv_all[z, x, y, c] = kv_out[mine]
 
-    pl.semaphore_wait(barrier, len(offsets) + (2 if Z > 1 else 0))
+    pl.semaphore_wait(barrier, len(offsets) + jnp.minimum(low, 1) + jnp.minimum(high, 1))
 
     def remote(src, dst, send, recv, to):
         return pltpu.make_async_remote_copy(
@@ -166,7 +167,12 @@
             device_id_type=pl.DeviceIdType.MESH,
         )
 
-    units_here = [((x + X - dx) % X, (y + Y - dy) % Y) for dx in range(X) for dy in range(Y)]
+    units_here = [
+        ((x + X - dx) % X, (y + Y - dy) % Y, (c + C - dc) % C)
+        for dx in range(X)
+        for dy in range(Y)
+        for dc in range(C)
+    ]
 
     def z_copy(at, upward, unit):
         return remote(
@@ -174,19 +180,12 @@
             kv_all.at[at, *unit],
             z_send.at[upward, at, *unit],
             z_recv.at[at, *unit],
-            device(x, c, (up if upward else down) * Y + y),
-        )
-
-    def goes(d, upward, j):
-        return d <= whole_way or (2 * d == Z and j % 2 == 1 - upward)
-
-    def pass_on(at, d, upward, j):
-        if isinstance(d, int):
-            if goes(d, upward, j):
-                z_copy(at, upward, units_here[j]).start()
-        else:
-            here = (d <= whole_way) | ((2 * d == Z) & (j % 2 == 1 - upward))
-            pl.when(here)(lambda: z_copy(at, upward, units_here[j]).start())
+            device(x, c, b + Y if upward else b - Y),
+        )
+
+    def pass_on(at, unit):
+        pl.when((at <= z) & (high > 0))(lambda: z_copy(at, 1, unit).start())
+        pl.when((at >= z) & (low > 0))(lambda: z_copy(at, 0, unit).start())
 
     def kv_copy(*offset):
         xx, yy, cc = member(*offset)
@@ -210,6 +209,7 @@
 
     for offset in offsets:
         kv_copy(*offset).start()
+    pass_on(z, units_here[0])
 
     loads[4].wait()
     q_heads = KVL * G
@@ -222,20 +222,15 @@
     q_all[x, :, y, c] = q_out[mine]
     for offset in offsets:
         q_copy(*offset).start()
-    for dx in range(X):
-        for dy in range(Y):
-            for dc in range(C):
-                if (dx, dy, dc) != (0, 0, 0):
-                    kv_copy(dx, dy, dc).wait_recv()
-            pass_on(z, 1, 1, dx * Y + dy)
-            pass_on(z, 1, 0, dx * Y + dy)
-
-    def receive(d):
-        for j, unit in enumerate(units_here):
-            z_copy(below(d), 1, unit).wait_recv()
-            pass_on(below(d), d + 1, 1, j)
-            z_copy(above(d), 0, unit).wait_recv()
-            pass_on(above(d), d + 1, 0, j)
+    for offset, unit in zip(offsets, units_here[1:]):
+        kv_copy(*offset).wait_recv()
+        pass_on(z, unit)
+
+    def receive(k):
+        at = z_near(k)
+        for unit in units_here:
+            z_copy(at, 1, unit).wait_recv()
+            pass_on(at, unit)
 
     scaling = math.log2(math.e) * D ** (-0.5)
 
@@ -374,40 +369,27 @@
             device(x, cc, z * Y + yy),
         )
 
-    if whole_way > 0:
-        receive(1)
+    small_loop(1, Z - 1, receive)
+    if Z > 1:
+        pl.when(between)(lambda: receive(Z - 1))
     for offset in offsets:
         q_copy(*offset).wait_recv()
-    attend([z] + [below(1), above(1)] * min(1, whole_way), True, Z == 1)
-
-    def later(d):
-        receive(d)
-        attend([below(d), above(d)], False, False)
-
-    small_loop(2, whole_way + 1, later)
-    if Z % 2 == 0:
-        opposite = above(Z // 2)
-        for j, unit in enumerate(units_here):
-            z_copy(opposite, 1 - j % 2, unit).wait_recv()
-        attend([opposite], False, True)
-    elif Z > 1:
-        attend([], False, True)
+    together = min(3, max(1, Z - 1))
+    attend([z_near(k) for k in range(together)], True, Z == 1)
+    small_loop(together, Z - 1, lambda k: attend([z_near(k)], False, False))
+    if Z > 1:
+        pl.when(jnp.logical_not(between))(lambda: receive(Z - 1))
+        attend([z_near(Z - 1)], False, True)
 
     for offset in offsets:
         kv_copy(*offset).wait_send()
         q_copy(*offset).wait_send()
-    def sent(d):
-        for j, unit in enumerate(units_here):
-            z_copy(below(d), 1, unit).wait_send()
-            z_copy(above(d), 0, unit).wait_send()
-
-    small_loop(0, whole_way, sent)
-    if Z % 2 == 0:
-        for j, unit in enumerate(units_here):
-            if j % 2 == 0:
-                z_copy(below(Z // 2 - 1), 1, unit).wait_send()
-            else:
-                z_copy(above(Z // 2 - 1), 0, unit).wait_send()
+    def sent(at):
+        for unit in units_here:
+            pl.when((at <= z) & (high > 0))(lambda: z_copy(at, 1, unit).wait_send())
+            pl.when((at >= z) & (low > 0))(lambda: z_copy(at, 0, unit).wait_send())
+
+    small_loop(0, Z, sent)
     for dx, dy, dc in offsets:
         if dx == 0:
             for piece in range(X):
@@ -453,8 +435,8 @@
             dma((X, Y, C)),
             dma((X, Y, C)),
             dma((X, Y, C)),
-            dma((2, Z, X, Y)),
-            dma((Z, X, Y)),
+            dma((2, Z, X, Y, C)),
+            dma((Z, X, Y, C)),
             dma((Y, C, X)),
             dma((Y, C, X)),
         ],

time: 25.5 us -> 26 us (1.020)
  Pallas kernels: 24.5 us -> 24.9 us
    pallas_call x1, Pallas kernels: 24.5 us -> 24.9 us  [per_device(): pl.pallas_call(functools.partial(attend_kernel, (X, C, Z, Y, R, KVL, G, D...]
where the time goes in v7:
time: 26 us; the launch traced here: 25.8 us
  Pallas kernels  24.9 us (96%)
  local copies, waits for them, and re-layouts  0.88 us (3%)
    pallas_call x1, Pallas kernels, per_device(): pl.pallas_call(functools.partial(attend_kernel, (X, C, Z, Y, R, KVL, G, D...  24.9 us
    reshape x1, local copies, waits for them, and re-layouts, per_device(): return jnp.transpose(out.reshape(Y * C * KVL * G, X * R, D), (1, 0, 2))  0.88 us

profile of v7, /device:TPU:0, one launch (start us, length us, event | category | flops | bytes accessed | tf_op | source)
XLA Modules:
  0.0 25.8 jit_solution(5854703129862883596)
XLA Ops:
  0.0 24.9 %shard_map.55 = bf16[4,1,4,64,128]{4,3,2,1,0:T(8,128)(2,1)S(1)} custom-call(s32[16]{0:T(128)} %run_hbm.1, f32[1,128]{1,0:T(1,128)} %constant.2.clone.freq_hbm, bf16[1,32,32,128]{3,2,1,0:T(8,128)(2,1)} %q_hbm.1, bf16[1,32,8,128]{3,2,1,0:T(8,128)(2,1)} %k_hbm.1, bf16[1,32,8,128]{3,2,1,0:T(8,128)(2,1)} %v_hbm.1), custom_call_target="tpu_custom_call" | custom-call | tf_op jit(solution)/shard_map/pallas_call | solution.py:413
  24.9 0.9 %copy.8 = bf16[16,64,128]{2,0,1:T(8,128)(2,1)} copy(bf16[16,64,128]{2,1,0:T(8,128)(2,1)S(1)} %bitcast.4) | data formatting | bytes 524288 | tf_op jit(solution)/shard_map/reshape | solution.py:447

commit v8 on v6

--- a/solution.py
+++ b/solution.py
@@ -213,11 +213,12 @@
 
     loads[4].wait()
     q_heads = KVL * G
-    for to in range(X * Y * C):
-        q_out[to] = (
-            rotated(by_head(q_ref, to * q_heads, q_heads))
+    share = math.gcd(X * Y * C, max(1, 8 // q_heads))
+    for to in range(0, X * Y * C, share):
+        q_out[to : to + share] = (
+            rotated(by_head(q_ref, to * q_heads, share * q_heads))
             .astype(jnp.bfloat16)
-            .reshape(KVL, G, R, D)
+            .reshape(share, KVL, G, R, D)
         )
     q_all[x, :, y, c] = q_out[mine]
     for offset in offsets:
@@ -282,7 +283,8 @@
 
         if planes:
             key_pos = {"early": key_positions(planes, early), "late": key_positions(planes, late)}
-        for dy in reversed(range(Y)):
+        def blocks_of(step, unused):
+            dy = Y - 1 - step
             yy = (y + dy) % Y
             for piece in range(X):
                 own = "early" if piece in early else "late"
@@ -358,11 +360,17 @@
                         sum_ref[piece, head, yy] = total
                         acc_ref[piece, head, yy] = update
                 if last:
-                    for dc in reversed(range(C)):
-                        if (dy, dc) != (0, 0):
-                            o_copy(dy, dc, piece).start()
-                        else:
-                            out_ref[y * C + c, :, :, pl.ds(piece * R, R)] = out_part[piece, y, c]
+                    for dc in range(1, C):
+                        o_copy(dy, dc, piece).start()
+
+                    def keep():
+                        out_ref[y * C + c, :, :, pl.ds(piece * R, R)] = out_part[piece, y, c]
+
+                    pl.when(dy > 0)(lambda: o_copy(dy, 0, piece).start())
+                    pl.when(dy == 0)(keep)
+            return unused
+
+        lax.fori_loop(0, Y, blocks_of, 0)
 
     def o_copy(dy, dc, piece):
         xx, yy, cc = member(0, dy, dc)

time: 25.5 us -> 25.6 us (level)
  no operation moved by 1% of the time
where the time goes in v8:
time: 25.6 us; the launch traced here: 25.4 us
  Pallas kernels  24.5 us (96%)
  local copies, waits for them, and re-layouts  0.88 us (3%)
    pallas_call x1, Pallas kernels, per_device(): pl.pallas_call(functools.partial(attend_kernel, (X, C, Z, Y, R, KVL, G, D...  24.5 us
    reshape x1, local copies, waits for them, and re-layouts, per_device(): return jnp.transpose(out.reshape(Y * C * KVL * G, X * R, D), (1, 0, 2))  0.88 us

profile of v8, /device:TPU:0, one launch (start us, length us, event | category | flops | bytes accessed | tf_op | source)
XLA Modules:
  0.0 25.4 jit_solution(11881043175027923489)
XLA Ops:
  0.0 24.5 %shard_map.55 = bf16[4,1,4,64,128]{4,3,2,1,0:T(8,128)(2,1)S(1)} custom-call(s32[16]{0:T(128)} %run_hbm.1, f32[1,128]{1,0:T(1,128)} %constant.2.clone.freq_hbm, bf16[1,32,32,128]{3,2,1,0:T(8,128)(2,1)} %q_hbm.1, bf16[1,32,8,128]{3,2,1,0:T(8,128)(2,1)} %k_hbm.1, bf16[1,32,8,128]{3,2,1,0:T(8,128)(2,1)} %v_hbm.1), custom_call_target="tpu_custom_call" | custom-call | tf_op jit(solution)/shard_map/pallas_call | solution.py:439
  24.5 0.9 %copy.8 = bf16[16,64,128]{2,0,1:T(8,128)(2,1)} copy(bf16[16,64,128]{2,1,0:T(8,128)(2,1)S(1)} %bitcast.4) | data formatting | bytes 524288 | tf_op jit(solution)/shard_map/reshape | solution.py:473

commit v9 on v8

--- a/solution.py
+++ b/solution.py
@@ -167,6 +167,7 @@
         )
 
     units_here = [((x + X - dx) % X, (y + Y - dy) % Y) for dx in range(X) for dy in range(Y)]
+    units_sorted = [(piece, (y + Y - dy) % Y) for piece in range(X) for dy in range(Y)]
 
     def z_copy(at, upward, unit):
         return remote(
@@ -180,13 +181,13 @@
     def goes(d, upward, j):
         return d <= whole_way or (2 * d == Z and j % 2 == 1 - upward)
 
-    def pass_on(at, d, upward, j):
+    def pass_on(at, d, upward, j, unit):
         if isinstance(d, int):
             if goes(d, upward, j):
-                z_copy(at, upward, units_here[j]).start()
+                z_copy(at, upward, unit).start()
         else:
             here = (d <= whole_way) | ((2 * d == Z) & (j % 2 == 1 - upward))
-            pl.when(here)(lambda: z_copy(at, upward, units_here[j]).start())
+            pl.when(here)(lambda: z_copy(at, upward, unit).start())
 
     def kv_copy(*offset):
         xx, yy, cc = member(*offset)
@@ -228,15 +229,15 @@
             for dc in range(C):
                 if (dx, dy, dc) != (0, 0, 0):
                     kv_copy(dx, dy, dc).wait_recv()
-            pass_on(z, 1, 1, dx * Y + dy)
-            pass_on(z, 1, 0, dx * Y + dy)
+            pass_on(z, 1, 1, dx * Y + dy, units_here[dx * Y + dy])
+            pass_on(z, 1, 0, dx * Y + dy, units_here[dx * Y + dy])
 
     def receive(d):
-        for j, unit in enumerate(units_here):
+        for j, unit in enumerate(units_sorted):
             z_copy(below(d), 1, unit).wait_recv()
-            pass_on(below(d), d + 1, 1, j)
+            pass_on(below(d), d + 1, 1, j, unit)
             z_copy(above(d), 0, unit).wait_recv()
-            pass_on(above(d), d + 1, 0, j)
+            pass_on(above(d), d + 1, 0, j, unit)
 
     scaling = math.log2(math.e) * D ** (-0.5)
 
@@ -267,7 +268,7 @@
     early = list(range(X // 2))
     late = list(range(X // 2, X))
 
-    def attend(planes, first, last):
+    def attend(planes, pieces_here, first, last):
 
         def units(kind, head, pieces):
             return jnp.concatenate(
@@ -286,7 +287,7 @@
         def blocks_of(step, unused):
             dy = Y - 1 - step
             yy = (y + dy) % Y
-            for piece in range(X):
+            for piece in pieces_here:
                 own = "early" if piece in early else "late"
                 parts = ["early"] if own == "early" else ["early", "late"]
                 for head in range(KVL):
@@ -386,32 +387,34 @@
         receive(1)
     for offset in offsets:
         q_copy(*offset).wait_recv()
-    attend([z] + [below(1), above(1)] * min(1, whole_way), True, Z == 1)
+    attend([z] + [below(1), above(1)] * min(1, whole_way), range(X), True, Z == 1)
 
     def later(d):
         receive(d)
-        attend([below(d), above(d)], False, False)
+        attend([below(d), above(d)], range(X), False, False)
 
     small_loop(2, whole_way + 1, later)
     if Z % 2 == 0:
         opposite = above(Z // 2)
-        for j, unit in enumerate(units_here):
-            z_copy(opposite, 1 - j % 2, unit).wait_recv()
-        attend([opposite], False, True)
+        for pieces in (early, late):
+            for j, unit in enumerate(units_sorted):
+                if j // Y in pieces:
+                    z_copy(opposite, 1 - j % 2, unit).wait_recv()
+            attend([opposite], pieces, False, True)
     elif Z > 1:
-        attend([], False, True)
+        attend([], range(X), False, True)
 
     for offset in offsets:
         kv_copy(*offset).wait_send()
         q_copy(*offset).wait_send()
     def sent(d):
-        for j, unit in enumerate(units_here):
+        for j, unit in enumerate(units_sorted):
             z_copy(below(d), 1, unit).wait_send()
             z_copy(above(d), 0, unit).wait_send()
 
     small_loop(0, whole_way, sent)
     if Z % 2 == 0:
-        for j, unit in enumerate(units_here):
+        for j, unit in enumerate(units_sorted):
             if j % 2 == 0:
                 z_copy(below(Z // 2 - 1), 1, unit).wait_send()
             else:

time: 25.6 us -> 24.7 us (0.965)
  Pallas kernels: 24.5 us -> 23.6 us
    pallas_call x1, Pallas kernels: 24.5 us -> 23.6 us  [per_device(): pl.pallas_call(functools.partial(attend_kernel, (X, C, Z, Y, R, KVL, G, D...]
where the time goes in v9:
time: 24.7 us; the launch traced here: 24.5 us
  Pallas kernels  23.6 us (96%)
  local copies, waits for them, and re-layouts  0.88 us (4%)
    pallas_call x1, Pallas kernels, per_device(): pl.pallas_call(functools.partial(attend_kernel, (X, C, Z, Y, R, KVL, G, D...  23.6 us
    reshape x1, local copies, waits for them, and re-layouts, per_device(): return jnp.transpose(out.reshape(Y * C * KVL * G, X * R, D), (1, 0, 2))  0.88 us

profile of v9, /device:TPU:0, one launch (start us, length us, event | category | flops | bytes accessed | tf_op | source)
XLA Modules:
  0.0 24.5 jit_solution(1823578431237427031)
XLA Ops:
  0.0 23.6 %shard_map.55 = bf16[4,1,4,64,128]{4,3,2,1,0:T(8,128)(2,1)S(1)} custom-call(s32[16]{0:T(128)} %run_hbm.1, f32[1,128]{1,0:T(1,128)} %constant.2.clone.freq_hbm, bf16[1,32,32,128]{3,2,1,0:T(8,128)(2,1)} %q_hbm.1, bf16[1,32,8,128]{3,2,1,0:T(8,128)(2,1)} %k_hbm.1, bf16[1,32,8,128]{3,2,1,0:T(8,128)(2,1)} %v_hbm.1), custom_call_target="tpu_custom_call" | custom-call | tf_op jit(solution)/shard_map/pallas_call | solution.py:442
  23.6 0.9 %copy.8 = bf16[16,64,128]{2,0,1:T(8,128)(2,1)} copy(bf16[16,64,128]{2,1,0:T(8,128)(2,1)S(1)} %bitcast.4) | data formatting | bytes 524288 | tf_op jit(solution)/shard_map/reshape | solution.py:476

commit v10 on v9

--- a/solution.py
+++ b/solution.py
@@ -178,16 +178,12 @@
             device(x, c, (up if upward else down) * Y + y),
         )
 
-    def goes(d, upward, j):
-        return d <= whole_way or (2 * d == Z and j % 2 == 1 - upward)
-
-    def pass_on(at, d, upward, j, unit):
-        if isinstance(d, int):
-            if goes(d, upward, j):
-                z_copy(at, upward, unit).start()
+    def pass_on(at, d, upward, unit):
+        relays = (d <= whole_way) | ((2 * d == Z) & (z % 2 == 1 - upward))
+        if isinstance(d, int) and d <= whole_way:
+            z_copy(at, upward, unit).start()
         else:
-            here = (d <= whole_way) | ((2 * d == Z) & (j % 2 == 1 - upward))
-            pl.when(here)(lambda: z_copy(at, upward, unit).start())
+            pl.when(relays)(lambda: z_copy(at, upward, unit).start())
 
     def kv_copy(*offset):
         xx, yy, cc = member(*offset)
@@ -229,15 +225,15 @@
             for dc in range(C):
                 if (dx, dy, dc) != (0, 0, 0):
                     kv_copy(dx, dy, dc).wait_recv()
-            pass_on(z, 1, 1, dx * Y + dy, units_here[dx * Y + dy])
-            pass_on(z, 1, 0, dx * Y + dy, units_here[dx * Y + dy])
+            pass_on(z, 1, 1, units_here[dx * Y + dy])
+            pass_on(z, 1, 0, units_here[dx * Y + dy])
 
     def receive(d):
-        for j, unit in enumerate(units_sorted):
+        for unit in units_sorted:
             z_copy(below(d), 1, unit).wait_recv()
-            pass_on(below(d), d + 1, 1, j, unit)
+            pass_on(below(d), d + 1, 1, unit)
             z_copy(above(d), 0, unit).wait_recv()
-            pass_on(above(d), d + 1, 0, j, unit)
+            pass_on(above(d), d + 1, 0, unit)
 
     scaling = math.log2(math.e) * D ** (-0.5)
 
@@ -399,7 +395,7 @@
         for pieces in (early, late):
             for j, unit in enumerate(units_sorted):
                 if j // Y in pieces:
-                    z_copy(opposite, 1 - j % 2, unit).wait_recv()
+                    z_copy(opposite, 1, unit).wait_recv()
             attend([opposite], pieces, False, True)
     elif Z > 1:
         attend([], range(X), False, True)
@@ -415,10 +411,8 @@
     small_loop(0, whole_way, sent)
     if Z % 2 == 0:
         for j, unit in enumerate(units_sorted):
-            if j % 2 == 0:
-                z_copy(below(Z // 2 - 1), 1, unit).wait_send()
-            else:
-                z_copy(above(Z // 2 - 1), 0, unit).wait_send()
+            pl.when(z % 2 == 0)(lambda: z_copy(below(Z // 2 - 1), 1, unit).wait_send())
+            pl.when(z % 2 == 1)(lambda: z_copy(above(Z // 2 - 1), 0, unit).wait_send())
     for dx, dy, dc in offsets:
         if dx == 0:
             for piece in range(X):

time: 24.7 us -> 24.7 us (level)
  no operation moved by 1% of the time
where the time goes in v10:
time: 24.7 us; the launch traced here: 24.5 us
  Pallas kernels  23.6 us (96%)
  local copies, waits for them, and re-layouts  0.88 us (4%)
    pallas_call x1, Pallas kernels, per_device(): pl.pallas_call(functools.partial(attend_kernel, (X, C, Z, Y, R, KVL, G, D...  23.6 us
    reshape x1, local copies, waits for them, and re-layouts, per_device(): return jnp.transpose(out.reshape(Y * C * KVL * G, X * R, D), (1, 0, 2))  0.88 us

profile of v10, /device:TPU:0, one launch (start us, length us, event | category | flops | bytes accessed | tf_op | source)
XLA Modules:
  0.0 24.5 jit_solution(4040373795208145751)
XLA Ops:
  0.0 23.6 %shard_map.55 = bf16[4,1,4,64,128]{4,3,2,1,0:T(8,128)(2,1)S(1)} custom-call(s32[16]{0:T(128)} %run_hbm.1, f32[1,128]{1,0:T(1,128)} %constant.2.clone.freq_hbm, bf16[1,32,32,128]{3,2,1,0:T(8,128)(2,1)} %q_hbm.1, bf16[1,32,8,128]{3,2,1,0:T(8,128)(2,1)} %k_hbm.1, bf16[1,32,8,128]{3,2,1,0:T(8,128)(2,1)} %v_hbm.1), custom_call_target="tpu_custom_call" | custom-call | tf_op jit(solution)/shard_map/pallas_call | solution.py:436
  23.6 0.9 %copy.8 = bf16[16,64,128]{2,0,1:T(8,128)(2,1)} copy(bf16[16,64,128]{2,1,0:T(8,128)(2,1)S(1)} %bitcast.4) | data formatting | bytes 524288 | tf_op jit(solution)/shard_map/reshape | solution.py:470

commit v11 on v10

--- a/solution.py
+++ b/solution.py
@@ -208,6 +208,15 @@
     for offset in offsets:
         kv_copy(*offset).start()
 
+    def forward(dx, dy):
+        for dc in range(C):
+            if (dx, dy, dc) != (0, 0, 0):
+                kv_copy(dx, dy, dc).wait_recv()
+        pass_on(z, 1, 1, units_here[dx * Y + dy])
+        pass_on(z, 1, 0, units_here[dx * Y + dy])
+
+    forward(0, 0)
+
     loads[4].wait()
     q_heads = KVL * G
     share = math.gcd(X * Y * C, max(1, 8 // q_heads))
@@ -222,11 +231,8 @@
         q_copy(*offset).start()
     for dx in range(X):
         for dy in range(Y):
-            for dc in range(C):
-                if (dx, dy, dc) != (0, 0, 0):
-                    kv_copy(dx, dy, dc).wait_recv()
-            pass_on(z, 1, 1, units_here[dx * Y + dy])
-            pass_on(z, 1, 0, units_here[dx * Y + dy])
+            if (dx, dy) != (0, 0):
+                forward(dx, dy)
 
     def receive(d):
         for unit in units_sorted:

time: 24.7 us -> 24 us (0.972)
  Pallas kernels: 23.6 us -> 22.9 us
    pallas_call x1, Pallas kernels: 23.6 us -> 22.9 us  [per_device(): pl.pallas_call(functools.partial(attend_kernel, (X, C, Z, Y, R, KVL, G, D...]
where the time goes in v11:
time: 24 us; the launch traced here: 23.8 us
  Pallas kernels  22.9 us (95%)
  local copies, waits for them, and re-layouts  0.88 us (4%)
    pallas_call x1, Pallas kernels, per_device(): pl.pallas_call(functools.partial(attend_kernel, (X, C, Z, Y, R, KVL, G, D...  22.9 us
    reshape x1, local copies, waits for them, and re-layouts, per_device(): return jnp.transpose(out.reshape(Y * C * KVL * G, X * R, D), (1, 0, 2))  0.88 us

profile of v11, /device:TPU:0, one launch (start us, length us, event | category | flops | bytes accessed | tf_op | source)
XLA Modules:
  0.0 23.8 jit_solution(12371012867323897813)
XLA Ops:
  0.0 22.9 %shard_map.55 = bf16[4,1,4,64,128]{4,3,2,1,0:T(8,128)(2,1)S(1)} custom-call(s32[16]{0:T(128)} %run_hbm.1, f32[1,128]{1,0:T(1,128)} %constant.2.clone.freq_hbm, bf16[1,32,32,128]{3,2,1,0:T(8,128)(2,1)} %q_hbm.1, bf16[1,32,8,128]{3,2,1,0:T(8,128)(2,1)} %k_hbm.1, bf16[1,32,8,128]{3,2,1,0:T(8,128)(2,1)} %v_hbm.1), custom_call_target="tpu_custom_call" | custom-call | tf_op jit(solution)/shard_map/pallas_call | solution.py:442
  22.9 0.9 %copy.8 = bf16[16,64,128]{2,0,1:T(8,128)(2,1)} copy(bf16[16,64,128]{2,1,0:T(8,128)(2,1)S(1)} %bitcast.4) | data formatting | bytes 524288 | tf_op jit(solution)/shard_map/reshape | solution.py:476
